TPU v7x, 256 devices: a whole 4x4x8 slice. The times are simulated.
256 devices in a mesh: ctx: 32 (over y, z), kvh: 8 (over x, core).
Axes of the slice: x: 4, y: 4, z: 8, core: 2. Of those that a mesh axis runs over, the one named last changes fastest.
Arguments:
- queries: bfloat16 [64, 64, 8, 1024], P('ctx', None, 'kvh'), may hold values from -92 to 92
- resp_keys: bfloat16 [64, 64, 8, 128], P('ctx', None, 'kvh'), may hold values from -6 to 6
- resp_values: bfloat16 [64, 64, 8, 128], P('ctx', None, 'kvh'), may hold values from -6 to 6
- prefix_keys: bfloat16 [32768, 8, 128], P('ctx', 'kvh'), may hold values from -6 to 6
- prefix_values: bfloat16 [32768, 8, 128], P('ctx', 'kvh'), may hold values from -6 to 6
- prefix_len: int32 [4], replicated, may hold values from 2048 to 8192, as said below
- prompt_of: int32 [64], replicated, may hold values from 0 to 3, as said below
- out_weight: bfloat16 [8192, 8192], P('kvh', 'ctx'), may hold values from -0.0625 to 0.0625
Outputs:
- attended: bfloat16 [64, 64, 8, 1024], P('ctx', None, 'kvh')
- projected: bfloat16 [4096, 8192], P('ctx', 'kvh')
Inputs may be any that keep to these rules, and one draw needn't show every extreme that they name: `prefix_len`: every prompt's length lies in the range and one prompt has exactly 8192. `prompt_of`: every prompt is named by 16 responses; the 2 responses of one index of ctx name each prompt at most 1 times, and some prompt exactly 1 times on every index.
All inputs are finite; a program needn't handle non-finite values.
Results may differ from a plain program's by a relative error of at most 0.038.
Values may be sent and summed in bfloat16 or wider, within the bound.
A program may use at most 128 MiB of HBM per device.

v0:
```python
import math

import jax
import jax.numpy as jnp
from jax import lax
from jax.sharding import PartitionSpec as P

MASKED = -1e30


def partial_block(query_rows, shard_keys, shard_values, live):
    scores = jnp.einsum(
        "bhd,sd->bhs", query_rows, shard_keys, preferred_element_type=jnp.float32
    ) * (1.0 / math.sqrt(shard_keys.shape[-1]))
    scores = jnp.where(live, scores, MASKED)
    peak_score = jnp.max(scores, axis=-1)
    weights = jnp.where(live, jnp.exp(scores - peak_score[..., None]), 0.0)
    totals = jnp.sum(weights, axis=-1)
    mixed_out = jnp.einsum(
        "bhs,sd->bhd",
        weights.astype(jnp.bfloat16),
        shard_values,
        preferred_element_type=jnp.float32,
    )
    return (mixed_out, peak_score, totals)


def holder_attend(incoming, shard_keys, shard_values, live_slots):
    sources, slot_rows, tokens_each, feature_width = incoming.shape
    head_size = shard_keys.shape[-1]
    head_count = feature_width // head_size
    total_rows = sources * slot_rows * tokens_each
    block_rows = math.gcd(512, total_rows)
    block_count = total_rows // block_rows
    stacked = incoming.reshape(block_count, block_rows, head_count, head_size)

    def one_block(query_rows):
        mixed_out, peak_score, totals = partial_block(
            query_rows, shard_keys, shard_values, live_slots[None, None, :]
        )
        return (
            mixed_out.astype(jnp.bfloat16).reshape(block_rows, feature_width),
            peak_score,
            totals,
        )

    mixed_out, peak_score, totals = lax.map(one_block, stacked)
    return (
        mixed_out.reshape(sources, slot_rows, tokens_each, feature_width),
        peak_score.reshape(sources, slot_rows, tokens_each, head_count),
        totals.reshape(sources, slot_rows, tokens_each, head_count),
    )


def return_partials(parts):
    return (
        lax.all_to_all(parts[0], "ctx", split_axis=0, concat_axis=0, tiled=True),
        lax.all_to_all(
            parts[1].astype(jnp.bfloat16), "ctx", split_axis=0, concat_axis=0, tiled=True
        ).astype(jnp.float32),
        lax.all_to_all(
            parts[2].astype(jnp.bfloat16), "ctx", split_axis=0, concat_axis=0, tiled=True
        ).astype(jnp.float32),
    )


def local(
    queries, resp_keys, resp_values, prefix_keys, prefix_values, prefix_len, prompt_of, out_weight
):
    ctx_count = lax.axis_size("ctx")
    position = lax.axis_index("ctx")
    own_queries = queries[:, :, 0]
    own_keys = resp_keys[:, :, 0]
    own_values = resp_values[:, :, 0]
    shard_keys = prefix_keys[:, 0]
    shard_values = prefix_values[:, 0]
    resp_count, tokens_each, feature_width = own_queries.shape
    slot_count, head_size = shard_keys.shape
    head_count = feature_width // head_size
    prompt_count = prefix_len.shape[0]
    holders = ctx_count // prompt_count
    capacity = max(1, resp_count // prompt_count)
    own_prompts = lax.dynamic_slice_in_dim(prompt_of, position * resp_count, resp_count, 0)
    local_ids = jnp.arange(resp_count, dtype=jnp.int32)
    same_prompt = own_prompts[None, :] == own_prompts[:, None]
    rank_within = jnp.sum(same_prompt & (local_ids[None, :] < local_ids[:, None]), axis=1)
    dest_prompt = jnp.arange(ctx_count, dtype=jnp.int32) // holders
    matches = (own_prompts[None, None, :] == dest_prompt[:, None, None]) & (
        rank_within[None, None, :] == jnp.arange(capacity, dtype=jnp.int32)[None, :, None]
    )
    chosen = jnp.sum(jnp.where(matches, local_ids[None, None, :], 0), axis=-1)
    present = jnp.any(matches, axis=-1)
    outgoing = jnp.where(
        present[:, :, None, None], own_queries[chosen], jnp.zeros((), jnp.bfloat16)
    )
    my_prompt = position // holders
    offset = position % holders * slot_count
    live_slots = offset + jnp.arange(slot_count, dtype=jnp.int32) < prefix_len[my_prompt]
    arrived = lax.all_to_all(outgoing, "ctx", split_axis=0, concat_axis=0, tiled=True)
    back_mixed, back_peak, back_totals = return_partials(
        holder_attend(arrived, shard_keys, shard_values, live_slots)
    )
    pick_rows = (
        own_prompts[:, None] * holders + jnp.arange(holders, dtype=jnp.int32)[None, :]
    ) * capacity + rank_within[:, None]
    got_mixed = back_mixed.reshape(ctx_count * capacity, tokens_each, feature_width)[pick_rows]
    got_peak = back_peak.reshape(ctx_count * capacity, tokens_each, head_count)[pick_rows]
    got_totals = back_totals.reshape(ctx_count * capacity, tokens_each, head_count)[pick_rows]
    own_rows = own_queries.reshape(resp_count, tokens_each, head_count, head_size)
    causal = jnp.arange(tokens_each)[:, None] >= jnp.arange(tokens_each)[None, :]
    own_mixed, own_peak, own_totals = jax.vmap(partial_block, in_axes=(0, 0, 0, None))(
        own_rows, own_keys, own_values, causal[:, None, :]
    )
    highest = jnp.maximum(own_peak, jnp.max(got_peak, axis=1))
    own_scale = jnp.exp(own_peak - highest)
    far_scale = jnp.exp(got_peak - highest[:, None])
    far_mixed = got_mixed.reshape(resp_count, holders, tokens_each, head_count, head_size).astype(
        jnp.float32
    )
    numerator = own_scale[..., None] * own_mixed + jnp.sum(far_scale[..., None] * far_mixed, axis=1)
    denominator = own_scale * own_totals + jnp.sum(far_scale * got_totals, axis=1)
    attended = (
        (numerator / denominator[..., None])
        .astype(jnp.bfloat16)
        .reshape(resp_count, tokens_each, feature_width)
    )
    flat_rows = attended.reshape(resp_count * tokens_each, feature_width)
    partial_terms = jnp.dot(
        flat_rows,
        lax.all_gather(out_weight, "ctx", axis=1, tiled=True),
        preferred_element_type=jnp.float32,
    )
    projected = lax.psum_scatter(
        partial_terms.astype(jnp.bfloat16), "kvh", scatter_dimension=1, tiled=True
    )
    return (attended[:, :, None, :], projected)


def solution(mesh):
    in_specs = (
        P("ctx", None, "kvh", None),
        P("ctx", None, "kvh", None),
        P("ctx", None, "kvh", None),
        P("ctx", "kvh", None),
        P("ctx", "kvh", None),
        P(),
        P(),
        P("kvh", "ctx"),
    )
    out_specs = (P("ctx", None, "kvh", None), P("ctx", "kvh"))
    return jax.shard_map(local, mesh=mesh, in_specs=in_specs, out_specs=out_specs, check_vma=False)
```

profile of v0, /device:TPU:1, one launch (start us, length us, event | category | flops | bytes accessed | tf_op | source)
XLA Modules:
  0.0 393.3 jit_solution(11850159908926039235)
XLA Ops:
  8.3 3.7 gather_fusion
  12.0 4.5 %bitcast_select_fusion = bf16[32,1,64,1024]{3,2,1,0:T(8,128)(2,1)} fusion(bf16[32,64,1024]{2,1,0:T(8,128)(2,1)} %gather_fusion, pred[32]{0:T(512)(128)(4,1)S(1)} %fusion.34), kind=kLoop, calls=%fused_computation.26 | loop fusion | flops 2097152 | bytes 8388640 | tf_op jit(solution)/shard_map/jit(_where)/select_n | solution.py:93
  16.5 12.3 %all-to-all-start = ((bf16[32,1,64,1024]{3,2,1,0:T(8,128)(2,1)}), bf16[32,1,64,1024]{3,2,1,0:T(8,128)(2,1)}, u32[]{:S(2)}, u32[]{:S(2)}) async-start(bf16[32,1,64,1024]{3,2,1,0:T(8,128)(2,1)} %bitcast_select_fusion), calls=%async_computation | async-start | bytes 8388608 | tf_op jit(solution)/shard_map/all_to_all | solution.py:99
  30.4 110.1 %all-to-all-done = bf16[32,1,64,1024]{3,2,1,0:T(8,128)(2,1)} async-done(((bf16[32,1,64,1024]{3,2,1,0:T(8,128)(2,1)}), bf16[32,1,64,1024]{3,2,1,0:T(8,128)(2,1)}, u32[]{:S(2)}, u32[]{:S(2)}) %all-to-all-start) | async-done | bytes 4194336 | tf_op jit(solution)/shard_map/all_to_all | solution.py:99
  140.5 5.2 %copy.98 = bf16[256,8,8,128]{3,2,1,0:T(8,128)(2,1)} copy(bf16[256,8,8,128]{3,1,2,0:T(8,128)(2,1)} %bitcast.44) | data formatting | bytes 8388608
  145.8 63.3 %while.15 = (s32[]{:T(128)}, bf16[4,512,1024]{2,1,0:T(8,128)(2,1)}, bf16[4,512,8]{1,2,0:T(8,128)(2,1)S(1)}, bf16[4,512,8]{1,2,0:T(8,128)(2,1)S(1)}, bf16[4,512,8...) while((s32[]{:T(128)}, bf16[4,512,1024]{2,1,0:T(8,128)(2,1)}, ...), condition=%wide.region_7.8_spmd.clone, body=%wide.region_4.7_spmd.clone.sunk | while | flops 2202527744 | bytes 59355768 | solution.py:47
  145.8 1.3 constant_dynamic-slice_fusion.2
  147.7 2.7 fusion.49
  150.4 4.7 %fusion.51 = bf16[512,8]{0,1:T(8,128)(2,1)S(1)} fusion(f32[512,8,1024]{2,0,1:T(8,128)S(1)} %get-tuple-element.224, f32[512,8]{0,1:T(8,128)S(1)} %get-tuple-element.225, pred[1024]{0:T(1024)(128)(4,1)S(1)} %add_compare_fusion.2), kind=kLoop, calls=%fused_computation.8.clone.1 | loop fusion | flops 20967424 | bytes 16802816 | tf_op jit(solution)/shard_map/while/body/eval_jaxpr/reduce_sum | solution.py:18
  155.1 4.8 %fusion.50 = bf16[512,8,128]{0,2,1:T(8,128)(2,1)S(1)} fusion(f32[512,8,1024]{2,0,1:T(8,128)S(1)} %get-tuple-element.224, f32[512,8]{0,1:T(8,128)S(1)} %get-tuple-element.225, pred[1024]{0:T(1024)(128)(4,1)S(1)} %add_compare_fusion.2, bf16[1024,128]{0,1:T(8,128)(2,1)S(1)} %get-tuple-element.252), kind=kOutput, calls=%fused_computation.12.clone.1 | convolution fusion | flops 1095237632 | bytes 18105344 | tf_op jit(solution)/shard_map/while/body/eval_jaxpr/bhs,sd->bhd/dot_general | solution.py:19
  160.5 1.1 constant_dynamic-update-slice_fusion.2
  161.7 1.3 constant_dynamic-slice_fusion.2
  163.6 2.7 fusion.49
  166.3 4.7 %fusion.51 = bf16[512,8]{0,1:T(8,128)(2,1)S(1)} fusion(f32[512,8,1024]{2,0,1:T(8,128)S(1)} %get-tuple-element.224, f32[512,8]{0,1:T(8,128)S(1)} %get-tuple-element.225, pred[1024]{0:T(1024)(128)(4,1)S(1)} %add_compare_fusion.2), kind=kLoop, calls=%fused_computation.8.clone.1 | loop fusion | flops 20967424 | bytes 16802816 | tf_op jit(solution)/shard_map/while/body/eval_jaxpr/reduce_sum | solution.py:18
  171.0 4.8 %fusion.50 = bf16[512,8,128]{0,2,1:T(8,128)(2,1)S(1)} fusion(f32[512,8,1024]{2,0,1:T(8,128)S(1)} %get-tuple-element.224, f32[512,8]{0,1:T(8,128)S(1)} %get-tuple-element.225, pred[1024]{0:T(1024)(128)(4,1)S(1)} %add_compare_fusion.2, bf16[1024,128]{0,1:T(8,128)(2,1)S(1)} %get-tuple-element.252), kind=kOutput, calls=%fused_computation.12.clone.1 | convolution fusion | flops 1095237632 | bytes 18105344 | tf_op jit(solution)/shard_map/while/body/eval_jaxpr/bhs,sd->bhd/dot_general | solution.py:19
  177.4 1.3 constant_dynamic-slice_fusion.2
  179.4 2.7 fusion.49
  182.1 4.7 %fusion.51 = bf16[512,8]{0,1:T(8,128)(2,1)S(1)} fusion(f32[512,8,1024]{2,0,1:T(8,128)S(1)} %get-tuple-element.224, f32[512,8]{0,1:T(8,128)S(1)} %get-tuple-element.225, pred[1024]{0:T(1024)(128)(4,1)S(1)} %add_compare_fusion.2), kind=kLoop, calls=%fused_computation.8.clone.1 | loop fusion | flops 20967424 | bytes 16802816 | tf_op jit(solution)/shard_map/while/body/eval_jaxpr/reduce_sum | solution.py:18
  186.8 4.8 %fusion.50 = bf16[512,8,128]{0,2,1:T(8,128)(2,1)S(1)} fusion(f32[512,8,1024]{2,0,1:T(8,128)S(1)} %get-tuple-element.224, f32[512,8]{0,1:T(8,128)S(1)} %get-tuple-element.225, pred[1024]{0:T(1024)(128)(4,1)S(1)} %add_compare_fusion.2, bf16[1024,128]{0,1:T(8,128)(2,1)S(1)} %get-tuple-element.252), kind=kOutput, calls=%fused_computation.12.clone.1 | convolution fusion | flops 1095237632 | bytes 18105344 | tf_op jit(solution)/shard_map/while/body/eval_jaxpr/bhs,sd->bhd/dot_general | solution.py:19
  193.2 1.3 constant_dynamic-slice_fusion.2
  195.2 2.7 fusion.49
  197.9 4.7 %fusion.51 = bf16[512,8]{0,1:T(8,128)(2,1)S(1)} fusion(f32[512,8,1024]{2,0,1:T(8,128)S(1)} %get-tuple-element.224, f32[512,8]{0,1:T(8,128)S(1)} %get-tuple-element.225, pred[1024]{0:T(1024)(128)(4,1)S(1)} %add_compare_fusion.2), kind=kLoop, calls=%fused_computation.8.clone.1 | loop fusion | flops 20967424 | bytes 16802816 | tf_op jit(solution)/shard_map/while/body/eval_jaxpr/reduce_sum | solution.py:18
  202.6 4.8 %fusion.50 = bf16[512,8,128]{0,2,1:T(8,128)(2,1)S(1)} fusion(f32[512,8,1024]{2,0,1:T(8,128)S(1)} %get-tuple-element.224, f32[512,8]{0,1:T(8,128)S(1)} %get-tuple-element.225, pred[1024]{0:T(1024)(128)(4,1)S(1)} %add_compare_fusion.2, bf16[1024,128]{0,1:T(8,128)(2,1)S(1)} %get-tuple-element.252), kind=kOutput, calls=%fused_computation.12.clone.1 | convolution fusion | flops 1095237632 | bytes 18105344 | tf_op jit(solution)/shard_map/while/body/eval_jaxpr/bhs,sd->bhd/dot_general | solution.py:19
  209.9 9.0 %all-to-all-start.1 = ((bf16[32,2,256]{2,1,0:T(2,128)(2,1)}), bf16[32,2,256]{2,1,0:T(2,128)(2,1)S(1)}, u32[]{:S(2)}, u32[]{:S(2)}) async-start(bf16[32,2,256]{2,1,0:T(2,128)(2,1)} %reshape.404), calls=%async_computation.1 | async-start | bytes 65536 | tf_op jit(solution)/shard_map/all_to_all | solution.py:58
  219.3 8.6 %all-to-all-done.1 = bf16[32,2,256]{2,1,0:T(2,128)(2,1)S(1)} async-done(((bf16[32,2,256]{2,1,0:T(2,128)(2,1)}), bf16[32,2,256]{2,1,0:T(2,128)(2,1)S(1)}, u32[]{:S(2)}, u32[]{:S(2)}) %all-to-all-start.1) | async-done | bytes 32800 | tf_op jit(solution)/shard_map/all_to_all | solution.py:58
  227.9 12.0 %all_to_all.20 = bf16[32,2,256]{2,1,0:T(2,128)(2,1)S(1)} all-to-all(bf16[32,2,256]{2,1,0:T(2,128)(2,1)S(1)} %reshape.406), channel_id=1, replica_groups=mesh['ctx'=32,'kvh'=8] {'ctx'}, dimensions={0} | all-to-all | bytes 65536 | tf_op jit(solution)/shard_map/all_to_all | solution.py:61
  239.9 5.0 %all-to-all-start.2 = ((bf16[32,1,64,1024]{3,2,1,0:T(8,128)(2,1)}), bf16[32,1,64,1024]{3,2,1,0:T(8,128)(2,1)}, u32[]{:S(2)}, u32[]{:S(2)}) async-start(bf16[32,1,64,1024]{3,2,1,0:T(8,128)(2,1)} %bitcast.130), calls=%async_computation.2 | async-start | bytes 8388608 | tf_op jit(solution)/shard_map/all_to_all | solution.py:57
  248.1 88.4 %all-to-all-done.2 = bf16[32,1,64,1024]{3,2,1,0:T(8,128)(2,1)} async-done(((bf16[32,1,64,1024]{3,2,1,0:T(8,128)(2,1)}), bf16[32,1,64,1024]{3,2,1,0:T(8,128)(2,1)}, u32[]{:S(2)}, u32[]{:S(2)}) %all-to-all-start.2) | async-done | bytes 4194336 | tf_op jit(solution)/shard_map/all_to_all | solution.py:57
  336.6 2.9 gather_fusion.2
  340.1 1.4 multiply_reduce_fusion
  342.0 9.5 %convolution_convert_fusion = bf16[128,8192]{1,0:T(8,128)(2,1)} fusion(bf16[1024,8192]{1,0:T(8,128)(2,1)} %all-gather.2.cloned.1.call-done, bf16[16,8,8,128]{3,2,1,0:T(8,128)(2,1)S(1)} %bitcast.131), kind=kOutput, calls=%fused_computation.25 | convolution fusion | flops 2148532224 | bytes 19136512 | tf_op jit(solution)/shard_map/dot_general | solution.py:128
  352.3 34.1 %reduce-scatter.2.cloned.1.call-done = bf16[128,1024]{1,0:T(8,128)(2,1)} async-done(((bf16[128,8192]{1,0:T(8,128)(2,1)}), bf16[128,1024]{1,0:T(8,128)(2,1)}) %reduce-scatter.2.cloned.1.call-update) | async-done | bytes 262160 | tf_op jit(solution)/shard_map/reduce_scatter | solution.py:133
  (82 shorter events, 16.9 us)
Async XLA Ops:
  7.2 334.3 %copy-start = (bf16[2,64,1,128]{3,1,2,0:T(8,128)(2,1)S(1)}, bf16[2,64,1,128]{3,1,2,0:T(8,128)(2,1)}, u32[]{:S(2)}) copy-start(bf16[2,64,1,128]{3,1,2,0:T(8,128)(2,1)} %param.12) | copy-start | bytes 98308
  16.5 13.1 %copy-start.3 = (bf16[1024,1,128]{2,0,1:T(8,128)(2,1)S(1)}, bf16[1024,1,128]{2,0,1:T(8,128)(2,1)}, u32[]{:S(2)}) copy-start(bf16[1024,1,128]{2,0,1:T(8,128)(2,1)} %param.14) | copy-start | bytes 786436
  16.5 13.3 %copy-start.5 = (s32[4]{0:T(128)S(1)}, s32[4]{0:T(128)}, u32[]{:S(2)}) copy-start(s32[4]{0:T(128)} %param.15) | copy-start | bytes 52
  16.5 124.0 %all-to-all-start = ((bf16[32,1,64,1024]{3,2,1,0:T(8,128)(2,1)}), bf16[32,1,64,1024]{3,2,1,0:T(8,128)(2,1)}, u32[]{:S(2)}, u32[]{:S(2)}) async-start(bf16[32,1,64,1024]{3,2,1,0:T(8,128)(2,1)} %bitcast_select_fusion), calls=%async_computation | async-start | bytes 8388608 | tf_op jit(solution)/shard_map/all_to_all | solution.py:99
  28.8 313.2 %all-gather.2.cloned.1.call-start = ((), (), s32[]{:S(2)}) async-start(), calls=%async_computation.5 | async-start | bytes 17301504 | tf_op jit(solution)/shard_map/all_gather | solution.py:130
  140.5 5.3 %copy-start.2 = (bf16[1024,1,128]{2,0,1:T(8,128)(2,1)S(1)}, bf16[1024,1,128]{2,0,1:T(8,128)(2,1)}, u32[]{:S(2)}) copy-start(bf16[1024,1,128]{2,0,1:T(8,128)(2,1)} %param.13) | copy-start | bytes 786436
  209.9 17.9 %all-to-all-start.1 = ((bf16[32,2,256]{2,1,0:T(2,128)(2,1)}), bf16[32,2,256]{2,1,0:T(2,128)(2,1)S(1)}, u32[]{:S(2)}, u32[]{:S(2)}) async-start(bf16[32,2,256]{2,1,0:T(2,128)(2,1)} %reshape.404), calls=%async_computation.1 | async-start | bytes 65536 | tf_op jit(solution)/shard_map/all_to_all | solution.py:58
  239.9 5.4 %copy-start.1 = (bf16[2,64,1,1024]{3,1,2,0:T(8,128)(2,1)S(1)}, bf16[2,64,1,1024]{3,1,2,0:T(8,128)(2,1)}, u32[]{:S(2)}) copy-start(bf16[2,64,1,1024]{3,1,2,0:T(8,128)(2,1)} %param.10) | copy-start | bytes 786436
  239.9 5.5 %copy-start.4 = (bf16[2,64,1,128]{3,1,2,0:T(8,128)(2,1)S(1)}, bf16[2,64,1,128]{3,1,2,0:T(8,128)(2,1)}, u32[]{:S(2)}) copy-start(bf16[2,64,1,128]{3,1,2,0:T(8,128)(2,1)} %param.11) | copy-start | bytes 98308
  239.9 96.7 %all-to-all-start.2 = ((bf16[32,1,64,1024]{3,2,1,0:T(8,128)(2,1)}), bf16[32,1,64,1024]{3,2,1,0:T(8,128)(2,1)}, u32[]{:S(2)}, u32[]{:S(2)}) async-start(bf16[32,1,64,1024]{3,2,1,0:T(8,128)(2,1)} %bitcast.130), calls=%async_computation.2 | async-start | bytes 8388608 | tf_op jit(solution)/shard_map/all_to_all | solution.py:57
  244.9 141.6 %reduce-scatter.2.cloned.1.call-start = ((), (), s32[]{:S(2)}) async-start(), calls=%async_computation.6 | async-start | bytes 2359296 | tf_op jit(solution)/shard_map/reduce_scatter | solution.py:133
Sparse Core Ops, SparseCore 0:
  32.1 207.9 all-gather.1
  351.7 34.7 reduce-scatter.1
where the time goes:
time: 396 us; the launch traced here: 393 us
  waiting for transfers between devices  242 us (61%)
  matrix products  40.4 us (10%)
  other arithmetic  29 us (7%)
  local copies, waits for them, and re-layouts  28.9 us (7%)
  starting transfers between devices  26.6 us (7%)
  between operations  14.4 us (4%)
  blocking collectives  12 us (3%)
    all_to_all x1, waiting for transfers between devices, local(): lax.all_to_all(outgoing, 'ctx', split_axis=0, concat_axis=0, tiled=True)  110 us
    all_to_all x1, waiting for transfers between devices, return_partials(): lax.all_to_all(parts[0], 'ctx', split_axis=0, concat_axis=0, tiled=True)  88.4 us
    reduce_scatter x1, waiting for transfers between devices, local(): lax.psum_scatter(partial_terms.astype(jnp.bfloat16), 'kvh', scatter_dimen...  34.1 us
    dot_general x5, matrix products, partial_block(): jnp.einsum('bhs,sd->bhd', weights.astype(jnp.bfloat16), shard_values, pre...  19.8 us
    reduce_sum x5, other arithmetic, partial_block(): totals = jnp.sum(weights, axis=-1)  19.1 us
    all_to_all x1, starting transfers between devices, local(): lax.all_to_all(outgoing, 'ctx', split_axis=0, concat_axis=0, tiled=True)  12.3 us
    all_to_all x1, blocking collectives, return_partials(): lax.all_to_all(parts[2].astype(jnp.bfloat16), 'ctx', split_axis=0, concat...  12 us
    dot_general x5, matrix products, partial_block(): jnp.einsum('bhd,sd->bhs', query_rows, shard_keys, preferred_element_type=...  11.1 us
  transfers between devices with their start and end apart: 5, of which 4 were waited for; matrix products, arithmetic and copies ran while one was open for 20% of the time, Pallas kernels for 0%

commit v1 on v0

v1 whole, which is shorter than its diff:
```python
import math

import jax
import jax.numpy as jnp
from jax import lax
from jax.experimental import pallas as pl
from jax.experimental.pallas import tpu as pltpu
from jax.sharding import PartitionSpec as P

MESH = pl.DeviceIdType.MESH
NY, NZ, NX = 4, 8, 4
TOK, HD, SLOTS = 64, 128, 1024
OWN = 2 * TOK
LINE = NZ * OWN
RANKS = 16
COLS = 256
MASKED = -1e30
SCALE2 = math.log2(math.e) / math.sqrt(HD)
TILE = 256
NT = (((1,), (1,)), ((), ()))
F32, BF16 = jnp.float32, jnp.bfloat16


def dot(a, b):
    return jnp.dot(a, b, preferred_element_type=F32)


def kernel(
    len_ref, prompt_ref, q_ref, rk_ref, rv_ref, k_ref, v_ref, w_ref,
    att_ref, proj_ref,
    src_tab, rank_tab,
    kv, qline, qsend, qarr, qh, acc, peak, own_o, own_lse, obuf, lbuf, osend, lsend, oarr, larr,
    abuf, wbuf, cacc, csend, crecv, xsend, xrecv, zsend, zrecv,
    local_sem, q1_s, q1_r, q2_s, q2_r, kv_s, kv_r, w_s, w_r, o_s, o_r, l_s, l_r, a_s, a_r, c_s, c_r, x_s, x_r, z_s, z_r,
):
    ctx, kvh = lax.axis_index("ctx"), lax.axis_index("kvh")
    y, z = lax.div(ctx, NZ), lax.rem(ctx, NZ)
    x, core = lax.div(kvh, 2), lax.rem(kvh, 2)
    sibling = x * 2 + 1 - core

    def z_at(d):
        return lax.rem(z + d + NZ, NZ)

    def y_at(d):
        return lax.rem(y + d, NY)

    def on_line(zz, head=None):
        return (y * NZ + zz, kvh if head is None else head)

    def on_column(yy):
        return (yy * NZ + z, kvh)

    def remote(src, dst, ss, rs, dev):
        return pltpu.make_async_remote_copy(
            src_ref=src, dst_ref=dst, send_sem=ss, recv_sem=rs, device_id=dev, device_id_type=MESH
        )

    locals_ = [
        pltpu.make_async_copy(src, dst, local_sem.at[i])
        for i, (src, dst) in enumerate([
            (k_ref, kv.at[0, 0, pl.ds(0, SLOTS)]),
            (rk_ref, kv.at[0, 0, pl.ds(SLOTS, OWN)]),
            (v_ref, kv.at[0, 1, pl.ds(0, SLOTS)]),
            (rv_ref, kv.at[0, 1, pl.ds(SLOTS, OWN)]),
            (q_ref.at[:, pl.ds(pl.multiple_of(z * HD, HD), HD)], qline.at[z]),
            (w_ref, wbuf.at[y]),
        ])
    ]
    for copy in locals_:
        copy.start()

    barrier = pltpu.get_barrier_semaphore()
    greeted = (
        [on_line(z_at(d)) for d in range(1, NZ)]
        + [on_line(z_at(d), sibling) for d in range(NZ)]
        + [on_column(y_at(d)) for d in range(1, NY)]
        + [(ctx, lax.rem(x + d, NX) * 2 + core) for d in range(1, NX)]
    )
    for dev in greeted:
        pl.semaphore_signal(barrier, inc=1, device_id=dev, device_id_type=MESH)
    pl.semaphore_wait(barrier, len(greeted))

    q1 = []
    for d in range(1, NZ):
        to = z_at(d)
        q1.append(remote(
            q_ref.at[:, pl.ds(pl.multiple_of(to * HD, HD), HD)], qline.at[z],
            q1_s.at[d - 1], q1_r.at[d - 1], on_line(to),
        ))
    for copy in q1:
        copy.start()

    right, left = on_line(z_at(1)), on_line(z_at(-1))

    def hop(src, dst, part, way):
        n = {1: 0, 2: 2, 3: 4, 4: 0, 5: 2, 6: 4, 7: 6}[dst] + (part if dst < 7 else 0)
        return remote(kv.at[src, part], kv.at[dst, part], kv_s.at[way, n], kv_r.at[way, n], left if way else right)

    hops = {}
    for part in range(2):
        for dst in range(1, 4):
            hops[dst, part] = hop(dst - 1, dst, part, 0)
        for dst in range(4, 7):
            hops[dst, part] = hop(0 if dst == 4 else dst - 1, dst, part, 1)
    hops[7, 0] = hop(3, 7, 0, 0)
    hops[7, 1] = hop(6, 7, 1, 1)

    for part in range(2):
        locals_[2 * part].wait()
        locals_[2 * part + 1].wait()
        hops[1, part].start()
        hops[4, part].start()

    run = jnp.int32(0)
    through = []
    for s in range(NY * NZ):
        named = (prompt_ref[2 * s] == y) | (prompt_ref[2 * s + 1] == y)
        rank_tab[s] = jnp.minimum(run, RANKS - 1)
        run = run + named.astype(jnp.int32)
        through.append(run)
    for j in range(RANKS):
        src = jnp.int32(0)
        for s in range(NY * NZ):
            src = src + (through[s] <= j).astype(jnp.int32)
        src_tab[j] = jnp.minimum(src, NY * NZ - 1)

    locals_[4].wait()
    for copy in q1:
        copy.wait_recv()

    def pick(zz, prompt):
        first = prompt_ref[(y * NZ + zz) * 2] == prompt
        return jnp.where(first, qline[zz, 0:TOK], qline[zz, TOK:OWN])

    q2 = []
    for d in range(1, NY):
        def fill(zz, carry, d=d):
            qsend[d - 1, zz] = pick(zz, y_at(d))
            return carry
        lax.fori_loop(0, NZ, fill, 0)
        copy = remote(
            qsend.at[d - 1], qarr.at[pl.ds(y * NZ, NZ)], q2_s.at[d - 1], q2_r.at[d - 1], on_column(y_at(d))
        )
        copy.start()
        q2.append(copy)

    def keep(zz, carry):
        qarr[y * NZ + zz] = pick(zz, y)
        return carry
    lax.fori_loop(0, NZ, keep, 0)

    locals_[5].wait()
    wy = [
        remote(wbuf.at[y], wbuf.at[y], w_s.at[d - 1], w_r.at[d - 1], on_column(y_at(d))) for d in range(1, NY)
    ]
    for copy in wy:
        copy.start()

    def own_block(slot, zz):
        scores = lax.dot_general(qline[zz], kv[slot, 0, SLOTS:SLOTS + OWN], NT, preferred_element_type=F32) * SCALE2
        row = lax.broadcasted_iota(jnp.int32, (OWN, OWN), 0)
        col = lax.broadcasted_iota(jnp.int32, (OWN, OWN), 1)
        live = (row >= col) & ((row < TOK) | (col >= TOK))
        scores = jnp.where(live, scores, MASKED)
        top = jnp.max(scores, axis=1, keepdims=True)
        weights = jnp.where(live, jnp.exp2(scores - top), 0.0)
        total = jnp.sum(weights, axis=1, keepdims=True)
        own_o[zz] = dot(weights.astype(BF16), kv[slot, 1, SLOTS:SLOTS + OWN]) / total
        own_lse[zz] = jnp.broadcast_to(top + jnp.log2(total), (OWN, HD))

    live_len = len_ref[y]
    ones = jnp.ones((SLOTS, HD), BF16)

    def attend(slot, block, first=False):
        live = block * SLOTS + lax.broadcasted_iota(jnp.int32, (1, SLOTS), 1) < live_len

        def tile(i, carry):
            rows = pl.ds(pl.multiple_of(i * TILE, TILE), TILE)
            scores = lax.dot_general(qh[rows], kv[slot, 0, 0:SLOTS], NT, preferred_element_type=F32)
            scores = jnp.where(live, scores * SCALE2, MASKED)
            top = jnp.max(scores, axis=1, keepdims=True)
            if not first:
                before = peak[rows]
                top = jnp.maximum(before[:, 0:1], top)
            weights = jnp.exp2(scores - top).astype(BF16)
            mixed = dot(weights, jnp.concatenate([kv[slot, 1, 0:SLOTS], ones], axis=1))
            top = jnp.broadcast_to(top, (TILE, HD))
            if not first:
                fade = jnp.exp2(before - top)
                mixed = mixed + acc[rows] * jnp.concatenate([fade, fade], axis=1)
            acc[rows] = mixed
            peak[rows] = top
            return carry
        lax.fori_loop(0, LINE // TILE, tile, 0)

    own_block(0, z)
    for copy in q2:
        copy.wait_recv()
    for j in range(RANKS):
        qh[j * TOK:(j + 1) * TOK] = qarr[src_tab[j]]
    attend(0, z, first=True)

    for step in range(1, 4):
        for part in range(2):
            for dst, after in ((step, step + 1 if step < 3 else 7), (step + 3, step + 4)):
                hops[dst, part].wait_recv()
                if step < 3 or part == (dst == 6):
                    hops[after, part].start()
        for slot, zz in ((step, z_at(-step)), (step + 3, z_at(step))):
            own_block(slot, zz)
            attend(slot, zz)
    for part in range(2):
        hops[7, part].wait_recv()
    own_block(7, z_at(4))
    attend(7, z_at(4))

    eye = lax.broadcasted_iota(jnp.int32, (TOK, HD), 0) == lax.broadcasted_iota(jnp.int32, (TOK, HD), 1)

    def finish(j, carry):
        rows = pl.ds(pl.multiple_of(j * TOK, TOK), TOK)
        total = acc[rows, HD:2 * HD]
        obuf[j] = (acc[rows, 0:HD] / total).astype(BF16)
        lse = jnp.sum(jnp.where(eye, peak[rows] + jnp.log2(total), 0.0), axis=0, keepdims=True)
        lbuf[j] = jnp.broadcast_to(lse, (8, HD))
        return carry
    lax.fori_loop(0, RANKS, finish, 0)

    back = []
    for d in range(1, NY):
        def put(zz, carry, d=d):
            rank = rank_tab[y_at(d) * NZ + zz]
            osend[d - 1, zz] = obuf[rank]
            lsend[d - 1, zz] = lbuf[rank]
            return carry
        lax.fori_loop(0, NZ, put, 0)
        back.append(remote(osend.at[d - 1], oarr.at[y], o_s.at[d - 1], o_r.at[d - 1], on_column(y_at(d))))
        back.append(remote(lsend.at[d - 1], larr.at[y], l_s.at[d - 1], l_r.at[d - 1], on_column(y_at(d))))
        back[-2].start()
        back[-1].start()

    def hold(zz, carry):
        rank = rank_tab[y * NZ + zz]
        oarr[y, zz] = obuf[rank]
        larr[y, zz] = lbuf[rank]
        return carry
    lax.fori_loop(0, NZ, hold, 0)
    for copy in back:
        copy.wait_recv()

    def merge(i, carry):
        zz, r = lax.div(i, 2), lax.rem(i, 2)
        prompt = prompt_ref[y * 2 * NZ + i]
        far = jnp.sum(jnp.where(eye, larr[prompt, zz, 0:1], 0.0), axis=1, keepdims=True)
        rows = pl.ds(pl.multiple_of(r * TOK, TOK), TOK)
        near = own_lse[zz, rows]
        top = jnp.maximum(far, near)
        far_w, near_w = jnp.exp2(far - top), jnp.exp2(near - top)
        both = oarr[prompt, zz].astype(F32) * far_w + own_o[zz, rows] * near_w
        abuf[0, pl.ds(pl.multiple_of(i * TOK, TOK), TOK)] = (both / (far_w + near_w)).astype(BF16)
        return carry
    lax.fori_loop(0, 2 * NZ, merge, 0)

    half = LINE // 2

    def a_hop(src, dst, part, way):
        n = {1: 0, 2: 2, 3: 4, 4: 0, 5: 2, 6: 4, 7: 6}[dst] + (part if dst < 7 else 0)
        rows = pl.ds(part * half, half)
        return remote(abuf.at[src, rows], abuf.at[dst, rows], a_s.at[way, n], a_r.at[way, n], left if way else right)

    a_hops = {}
    for part in range(2):
        for dst in range(1, 4):
            a_hops[dst, part] = a_hop(dst - 1, dst, part, 0)
        for dst in range(4, 7):
            a_hops[dst, part] = a_hop(0 if dst == 4 else dst - 1, dst, part, 1)
    a_hops[7, 0] = a_hop(3, 7, 0, 0)
    a_hops[7, 1] = a_hop(6, 7, 1, 1)
    for part in range(2):
        a_hops[1, part].start()
        a_hops[4, part].start()

    for copy in wy:
        copy.wait_recv()

    def project(slots, heads, first=False):
        for slot, head in zip(slots, heads):
            att_ref[:, pl.ds(pl.multiple_of(head * HD, HD), HD)] = abuf[slot, pl.ds(pl.multiple_of(z * OWN, OWN), OWN)]

        def tile(i, carry):
            rows = pl.ds(pl.multiple_of(i * TILE, TILE), TILE)
            a = jnp.concatenate([abuf[slot, rows] for slot in slots], axis=1)
            for yy in range(NY):
                w = jnp.concatenate(
                    [wbuf[yy, pl.ds(pl.multiple_of(head * HD, HD), HD)] for head in heads], axis=0
                )
                term = dot(a, w)
                cols = slice(yy * COLS, (yy + 1) * COLS)
                cacc[rows, cols] = term if first else cacc[rows, cols] + term
            return carry
        lax.fori_loop(0, LINE // TILE, tile, 0)

    project([0], [z], first=True)
    for step in range(1, 4):
        for part in range(2):
            for dst, after in ((step, step + 1 if step < 3 else 7), (step + 3, step + 4)):
                a_hops[dst, part].wait_recv()
                if step < 3 or part == (dst == 6):
                    a_hops[after, part].start()
        project([step, step + 3], [z_at(-step), z_at(step)])
    for part in range(2):
        a_hops[7, part].wait_recv()
    project([7], [z_at(4)])

    csend[...] = cacc[pl.ds(pl.multiple_of(core * half, half), half)].astype(BF16)
    across = remote(csend, crecv, c_s, c_r, (ctx, sibling))
    across.start()
    across.wait_recv()
    for xx in range(NX):
        cols = slice(xx * COLS, (xx + 1) * COLS)
        kept = cacc[pl.ds(pl.multiple_of((1 - core) * half, half), half), cols]
        xsend[xx] = (kept + crecv[:, cols].astype(F32)).astype(BF16)

    xs = []
    for d in range(1, NX):
        to = lax.rem(x + d, NX)
        xs.append(remote(xsend.at[to], xrecv.at[d - 1], x_s.at[d - 1], x_r.at[d - 1], (ctx, to * 2 + core)))
        xs[-1].start()
    for copy in xs:
        copy.wait_recv()
    summed = xsend[x].astype(F32)
    for d in range(NX - 1):
        summed = summed + xrecv[d].astype(F32)
    zsend[...] = summed.astype(BF16).reshape(NZ // 2, OWN, COLS)

    quarter = NZ // 2
    upper, place = lax.div(z, quarter), lax.rem(z, quarter)
    zs = []
    for d in range(quarter):
        to = lax.rem(place + d, quarter)
        zs.append(remote(
            zsend.at[to], zrecv.at[place], z_s.at[d], z_r.at[d], on_line((1 - core) * quarter + to, x * 2 + upper)
        ))
        zs[-1].start()
    for copy in zs:
        copy.wait_recv()
    for i in range(quarter):
        proj_ref[:, i * COLS:(i + 1) * COLS] = zrecv[i]

    for copy in q1 + q2 + wy + back + xs + zs + [across] + list(hops.values()) + list(a_hops.values()):
        copy.wait_send()


def local(queries, resp_keys, resp_values, prefix_keys, prefix_values, prefix_len, prompt_of, out_weight):
    dma = pltpu.SemaphoreType.DMA
    smem, vmem, any_ = pltpu.SMEM, pltpu.VMEM, pl.ANY
    attended, projected = pl.pallas_call(
        kernel,
        out_shape=(
            jax.ShapeDtypeStruct((OWN, NZ * HD), BF16),
            jax.ShapeDtypeStruct((OWN, NX * COLS), BF16),
        ),
        in_specs=[pl.BlockSpec(memory_space=smem)] * 2 + [pl.BlockSpec(memory_space=any_)] * 6,
        out_specs=(pl.BlockSpec(memory_space=vmem), pl.BlockSpec(memory_space=vmem)),
        scratch_shapes=[
            smem((RANKS,), jnp.int32),
            smem((NY * NZ,), jnp.int32),
            vmem((NZ, 2, SLOTS + OWN, HD), BF16),
            vmem((NZ, OWN, HD), BF16),
            vmem((NY - 1, NZ, TOK, HD), BF16),
            vmem((NY * NZ, TOK, HD), BF16),
            vmem((LINE, HD), BF16),
            vmem((LINE, 2 * HD), F32),
            vmem((LINE, HD), F32),
            vmem((NZ, OWN, HD), F32),
            vmem((NZ, OWN, HD), F32),
            vmem((RANKS, TOK, HD), BF16),
            vmem((RANKS, 8, HD), F32),
            vmem((NY - 1, NZ, TOK, HD), BF16),
            vmem((NY - 1, NZ, 8, HD), F32),
            vmem((NY, NZ, TOK, HD), BF16),
            vmem((NY, NZ, 8, HD), F32),
            vmem((NZ, LINE, HD), BF16),
            vmem((NY, NZ * HD, COLS), BF16),
            vmem((LINE, NY * COLS), F32),
            vmem((LINE // 2, NY * COLS), BF16),
            vmem((LINE // 2, NY * COLS), BF16),
            vmem((NX, LINE // 2, COLS), BF16),
            vmem((NX - 1, LINE // 2, COLS), BF16),
            vmem((NZ // 2, OWN, COLS), BF16),
            vmem((NZ // 2, OWN, COLS), BF16),
            dma((6,)),
            dma((NZ - 1,)), dma((NZ - 1,)),
            dma((NY - 1,)), dma((NY - 1,)),
            dma((2, 7)), dma((2, 7)),
            dma((NY - 1,)), dma((NY - 1,)),
            dma((NY - 1,)), dma((NY - 1,)),
            dma((NY - 1,)), dma((NY - 1,)),
            dma((2, 7)), dma((2, 7)),
            dma, dma,
            dma((NX - 1,)), dma((NX - 1,)),
            dma((NZ // 2,)), dma((NZ // 2,)),
        ],
        compiler_params=pltpu.CompilerParams(
            collective_id=0, has_side_effects=True, vmem_limit_bytes=48 * 1024 * 1024
        ),
        cost_estimate=pl.CostEstimate(flops=7_000_000_000, bytes_accessed=3_000_000, transcendentals=9_000_000),
    )(
        prefix_len,
        prompt_of,
        queries.reshape(OWN, NZ * HD),
        resp_keys.reshape(OWN, HD),
        resp_values.reshape(OWN, HD),
        prefix_keys.reshape(SLOTS, HD),
        prefix_values.reshape(SLOTS, HD),
        out_weight,
    )
    return (attended.reshape(2, TOK, 1, NZ * HD), projected)


def solution(mesh):
    in_specs = (
        P("ctx", None, "kvh", None),
        P("ctx", None, "kvh", None),
        P("ctx", None, "kvh", None),
        P("ctx", "kvh", None),
        P("ctx", "kvh", None),
        P(),
        P(),
        P("kvh", "ctx"),
    )
    out_specs = (P("ctx", None, "kvh", None), P("ctx", "kvh"))
    return jax.shard_map(local, mesh=mesh, in_specs=in_specs, out_specs=out_specs, check_vma=False)
```

time: 396 us -> 139 us (0.35)
  waiting for transfers between devices: 242 us -> 0 us
  Pallas kernels: 0 us -> 131 us
  matrix products: 40.4 us -> 0 us
  other arithmetic: 29 us -> 0 us
  starting transfers between devices: 26.6 us -> 0 us
  local copies, waits for them, and re-layouts: 28.9 us -> 7.47 us
  between operations: 14.4 us -> 0.66 us
  blocking collectives: 12 us -> 0 us
    all_to_all x3 -> x0, waiting for transfers between devices: 207 us -> none  [the longest x1 110 us: local(): lax.all_to_all(outgoing, 'ctx', split_axis=0, concat_axis=0, tiled=True)]
    pallas_call x0 -> x1, Pallas kernels: none -> 131 us  [local(): pl.pallas_call(kernel, out_shape=(jax.ShapeDtypeStruct((OWN, NZ * HD), BF...]
    dot_general x11 -> x0, matrix products: 40.4 us -> none  [the longest x5 19.8 us: partial_block(): jnp.einsum('bhs,sd->bhd', weights.astype(jnp.bfloat16), shard_values, pre...]
    reduce_scatter x1 -> x0, waiting for transfers between devices: 34.1 us -> none  [local(): lax.psum_scatter(partial_terms.astype(jnp.bfloat16), 'kvh', scatter_dimen...]
    all_to_all x3 -> x0, starting transfers between devices: 26.3 us -> none  [the longest x1 12.3 us: local(): lax.all_to_all(outgoing, 'ctx', split_axis=0, concat_axis=0, tiled=True)]
    reduce_sum x9 -> x0, other arithmetic: 20.8 us -> none  [the longest x5 19.1 us: partial_block(): totals = jnp.sum(weights, axis=-1)]
    all_to_all x1 -> x0, blocking collectives: 12 us -> none  [return_partials(): lax.all_to_all(parts[2].astype(jnp.bfloat16), 'ctx', split_axis=0, concat...]
    gather x4 -> x0, local copies, waits for them, and re-layouts: 7.69 us -> none  [the longest x1 3.69 us: local(): own_queries[chosen]]
  transfers between devices with their start and end apart: 5 -> 0, of which waited for: 4 -> 0; matrix products, arithmetic and copies ran while one was open for 20% -> 0% of each run, Pallas kernels for 0% -> 0%
where the time goes in v1:
time: 139 us
  Pallas kernels  131 us (94%)
  local copies, waits for them, and re-layouts  7.47 us (5%)
    pallas_call x1, Pallas kernels, local(): pl.pallas_call(kernel, out_shape=(jax.ShapeDtypeStruct((OWN, NZ * HD), BF...  131 us
    unnamed x18, local copies, waits for them, and re-layouts  7.47 us

profile of v1, /device:TPU:1, one launch (start us, length us, event | category | flops | bytes accessed | tf_op | source)
XLA Modules:
  0.0 139.1 jit_solution(11462931960092434576)
XLA Ops:
  0.6 0.0 copy-start.6
  0.6 0.0 copy-start.7
  0.7 0.6 copy-done.6
  1.3 0.0 copy-done.7
  1.3 0.0 copy-start
  1.3 1.0 copy-done
  2.3 0.0 copy-start.1
  2.3 0.9 copy-done.1
  3.3 0.0 copy-start.2
  3.3 0.9 copy-done.2
  4.2 0.0 copy-start.3
  4.2 0.9 copy-done.3
  5.2 0.0 copy-start.4
  5.2 0.8 copy-done.4
  6.0 0.0 copy-start.5
  6.0 0.8 copy-done.5
  6.7 131.0 %shard_map.95 = (bf16[128,1024]{1,0:T(8,128)(2,1)S(1)}, bf16[128,1024]{1,0:T(8,128)(2,1)S(1)}) custom-call(s32[4]{0:T(128)S(1)} %copy-done.6, s32[64]{0:T(128)S(1)} %copy-done.7, bf16[128,1024]{1,0:T(8,128)(2,1)S(1)} %bitcast.9, bf16[128,128]{1,0:T(8,128)(2,1)S(1)} %bitcast.12, bf16[128,128]{1,0:T(8,128)(2,1)S(1)} %bitcast.13, ...), custom_call_target="tpu_custom_call" | custom-call | flops 7000000000 | bytes 3000000 | tf_op jit(solution)/shard_map/pallas_call | solution.py:356
  137.7 0.7 copy.13
  138.4 0.7 copy.14
Async XLA Ops:
  0.6 0.7 copy-start.6
  0.6 0.7 copy-start.7
  1.3 1.0 copy-start
  2.3 0.9 copy-start.1
  3.3 0.9 copy-start.2
  4.2 0.9 copy-start.3
  5.2 0.8 copy-start.4
  6.0 0.8 copy-start.5

commit v2 on v0

v2 whole, which is shorter than its diff:
```python
import math

import jax
import jax.numpy as jnp
from jax import lax
from jax.experimental import pallas as pl
from jax.experimental.pallas import tpu as pltpu
from jax.sharding import PartitionSpec as P

MESH = pl.DeviceIdType.MESH
NY, NZ, NX = 4, 8, 4
TOK, HD, SLOTS = 64, 128, 1024
OWN = 2 * TOK
RANKS = 16
CH, CT = 4, 16
CR = RANKS * CT
COLS = 256
HALF = CR // 2
QUARTER = NZ // 2
PIECE = 2 * CT
MASKED = -1e30
SCALE2 = math.log2(math.e) / math.sqrt(HD)
NT = (((1,), (1,)), ((), ()))
F32, BF16 = jnp.float32, jnp.bfloat16


def dot(a, b):
    return jnp.dot(a, b, preferred_element_type=F32)


def iota(shape, dim):
    return lax.broadcasted_iota(jnp.int32, shape, dim)


def kernel(
    len_in, prompt_in, q_in, rk_in, rv_in, k_in, v_in, w_in,
    att_ref, proj_ref,
    len_ref, prompt_ref, src_tab, rank_tab,
    qall, okv, kv, qline, qsend, qarr, qh, acc, peak, own_o, own_l, own_oarr, own_larr,
    obuf, lbuf, osend, lsend, oarr0, oarr1, oarr2, oarr3, larr0, larr1, larr2, larr3, abuf, wbuf, cbuf, csend, crecv, xsend, xrecv, zsend, zrecv,
    local_s, q1_s, q1_r, q2_s, q2_r, kv_s, kv_r, w_s, w_r, own_s, own_r, o_s, o_r, l_s, l_r, a_s, a_r,
    c_s, c_r, x_s, x_r, z_s, z_r,
):
    ctx, kvh = lax.axis_index("ctx"), lax.axis_index("kvh")
    y, z = lax.div(ctx, NZ), lax.rem(ctx, NZ)
    x, core = lax.div(kvh, 2), lax.rem(kvh, 2)
    upper, place = lax.div(z, QUARTER), lax.rem(z, QUARTER)
    sibling = x * 2 + 1 - core
    started = []
    oarr, larr = (oarr0, oarr1, oarr2, oarr3), (larr0, larr1, larr2, larr3)

    def z_at(d):
        return lax.rem(z + d + NZ, NZ)

    def y_at(d):
        return lax.rem(y + d, NY)

    def on_line(zz, head=None):
        return (y * NZ + zz, kvh if head is None else head)

    def on_column(yy):
        return (yy * NZ + z, kvh)

    def remote(src, dst, ss, rs, dev):
        return pltpu.make_async_remote_copy(
            src_ref=src, dst_ref=dst, send_sem=ss, recv_sem=rs, device_id=dev, device_id_type=MESH
        )

    def start(copy):
        copy.start()
        started.append(copy)
        return copy

    locals_ = [
        pltpu.make_async_copy(src, dst, local_s.at[i])
        for i, (src, dst) in enumerate([
            (k_in, kv.at[0, 0]),
            (v_in, kv.at[0, 1]),
            (q_in, qall),
            (rk_in, okv.at[0]),
            (rv_in, okv.at[1]),
            (w_in, wbuf.at[y]),
            (len_in, len_ref),
            (prompt_in, prompt_ref),
        ])
    ]
    for copy in locals_:
        copy.start()

    barrier = pltpu.get_barrier_semaphore()
    greeted = (
        [on_line(z_at(d)) for d in range(1, NZ)]
        + [on_line(upper * QUARTER + i, sibling) for i in range(QUARTER)]
        + [on_column(y_at(d)) for d in range(1, NY)]
        + [(ctx, lax.rem(x + d, NX) * 2 + core) for d in range(1, NX)]
    )
    for dev in greeted:
        pl.semaphore_signal(barrier, inc=1, device_id=dev, device_id_type=MESH)
    for copy in locals_:
        copy.wait()
    pl.semaphore_wait(barrier, len(greeted))

    def head_cols(head):
        return pl.ds(pl.multiple_of(head * HD, HD), HD)

    q1 = [
        start(remote(
            qall.at[:, head_cols(z_at(d))], qline.at[z], q1_s.at[d - 1], q1_r.at[d - 1], on_line(z_at(d))
        ))
        for d in range(1, NZ)
    ]

    right, left = on_line(z_at(1)), on_line(z_at(-1))

    def slots_of(step, way):
        before = 0 if step == 1 else step - 1 + 3 * way
        return before, 7 if step == 4 else step + 3 * way

    def hop(step, part, way):
        src, dst = slots_of(step, way)
        return remote(
            kv.at[src, part], kv.at[dst, part], kv_s.at[way, part, step - 1], kv_r.at[way, part, step - 1],
            left if way else right,
        )

    hops = {(step, part, way): hop(step, part, way) for step in range(1, 4) for part in range(2) for way in range(2)}
    hops[4, 0, 0] = hop(4, 0, 0)
    hops[4, 1, 1] = hop(4, 1, 1)

    def forward(step, part):
        for way in range(2):
            hops[step, part, way].wait_recv()
            if (step + 1, part, way) in hops:
                start(hops[step + 1, part, way])

    for part in range(2):
        for way in range(2):
            start(hops[1, part, way])

    run = jnp.int32(0)
    through = []
    for s in range(NY * NZ):
        named = (prompt_ref[2 * s] == y) | (prompt_ref[2 * s + 1] == y)
        rank_tab[s] = jnp.minimum(run, RANKS - 1)
        run = run + named.astype(jnp.int32)
        through.append(run)
    for j in range(RANKS):
        src = jnp.int32(0)
        for s in range(NY * NZ):
            src = src + (through[s] <= j).astype(jnp.int32)
        src_tab[j] = jnp.minimum(src, NY * NZ - 1)

    def own_block(head, carry):
        scores = lax.dot_general(qall[:, head_cols(head)], okv[0], NT, preferred_element_type=F32) * SCALE2
        row, col = iota((OWN, OWN), 0), iota((OWN, OWN), 1)
        live = (row >= col) & ((row < TOK) | (col >= TOK))
        scores = jnp.where(live, scores, MASKED)
        top = jnp.max(scores, axis=1, keepdims=True)
        weights = jnp.where(live, jnp.exp2(scores - top), 0.0)
        total = jnp.sum(weights, axis=1, keepdims=True)
        own_o[head] = (dot(weights.astype(BF16), okv[1]) / total).astype(BF16)
        lse = jnp.sum(jnp.where(row == col, top + jnp.log2(total), 0.0), axis=0, keepdims=True)
        own_l[head] = jnp.broadcast_to(lse, (8, HD))
        return carry
    lax.fori_loop(0, NZ, own_block, 0)
    own_oarr[z] = own_o[z]
    own_larr[z] = own_l[z]

    qline[z] = qall[:, head_cols(z)]
    for copy in q1:
        copy.wait_recv()

    def pick(zz, prompt):
        first = prompt_ref[(y * NZ + zz) * 2] == prompt
        return jnp.where(first, qline[zz, 0:TOK], qline[zz, TOK:OWN])

    q2 = []
    for d in range(1, NY):
        def fill(zz, carry, d=d):
            qsend[d - 1, zz] = pick(zz, y_at(d))
            return carry
        lax.fori_loop(0, NZ, fill, 0)
        q2.append(start(remote(
            qsend.at[d - 1], qarr.at[pl.ds(y * NZ, NZ)], q2_s.at[d - 1], q2_r.at[d - 1], on_column(y_at(d))
        )))

    def keep(zz, carry):
        qarr[y * NZ + zz] = pick(zz, y)
        return carry
    lax.fori_loop(0, NZ, keep, 0)

    wy = [
        start(remote(wbuf.at[y], wbuf.at[y], w_s.at[d - 1], w_r.at[d - 1], on_column(y_at(d))))
        for d in range(1, NY)
    ]

    live_len = len_ref[y]
    ones = jnp.ones((SLOTS, HD), BF16)

    def attend(slot, block, chunk, first=False):
        rows = slice(chunk * CR, (chunk + 1) * CR)
        live = block * SLOTS + iota((1, SLOTS), 1) < live_len
        scores = lax.dot_general(qh[rows], kv[slot, 0], NT, preferred_element_type=F32)
        scores = jnp.where(live, scores * SCALE2, MASKED)
        top = jnp.max(scores, axis=1, keepdims=True)
        if not first:
            before = peak[rows]
            top = jnp.maximum(before[:, 0:1], top)
        weights = jnp.exp2(scores - top).astype(BF16)
        mixed = dot(weights, jnp.concatenate([kv[slot, 1], ones], axis=1))
        top = jnp.broadcast_to(top, (CR, HD))
        if not first:
            fade = jnp.exp2(before - top)
            mixed = mixed + acc[rows] * jnp.concatenate([fade, fade], axis=1)
        acc[rows] = mixed
        peak[rows] = top

    def attend_both(step):
        def body(way, carry):
            for chunk in range(CH):
                attend(step + 3 * way, z_at(step * (2 * way - 1)), chunk)
            return carry
        lax.fori_loop(0, 2, body, 0)

    forward(1, 0)
    for copy in q2:
        copy.wait_recv()
    for j in range(RANKS):
        rows = qarr[src_tab[j]]
        for chunk in range(CH):
            qh[chunk * CR + j * CT:chunk * CR + (j + 1) * CT] = rows[chunk * CT:(chunk + 1) * CT]
    for chunk in range(CH):
        attend(0, z, chunk, first=True)
    forward(1, 1)
    attend_both(1)
    forward(2, 0)
    forward(2, 1)
    attend_both(2)
    forward(3, 0)
    forward(3, 1)
    owns = []
    for d in range(1, NZ):
        to = z_at(d)
        owns.append(start(remote(own_o.at[to], own_oarr.at[z], own_s.at[0, d - 1], own_r.at[0, d - 1], on_line(to))))
        owns.append(start(remote(own_l.at[to], own_larr.at[z], own_s.at[1, d - 1], own_r.at[1, d - 1], on_line(to))))
    attend_both(3)
    hops[4, 0, 0].wait_recv()
    hops[4, 1, 1].wait_recv()

    eye = iota((CT, HD), 0) == iota((CT, HD), 1)
    sub = iota((8, HD), 0)

    def finish(chunk):
        first = chunk * CR
        total = acc[first:first + CR, HD:2 * HD]
        out = (acc[first:first + CR, 0:HD] / total).astype(BF16)
        lse = peak[first:first + CR] + jnp.log2(total)
        for j in range(RANKS):
            obuf[chunk, j] = out[j * CT:(j + 1) * CT]
            row = jnp.sum(jnp.where(eye, lse[j * CT:(j + 1) * CT], 0.0), axis=0, keepdims=True)
            lbuf[chunk, j] = jnp.broadcast_to(row, (8, HD))

    back = {}

    def put(chunk, d):
        lines = jnp.zeros((8, HD), F32)
        for zz in range(NZ):
            rank = rank_tab[y_at(d) * NZ + zz]
            lines = jnp.where(sub == zz, lbuf[chunk, rank], lines)
            if d:
                osend[d - 1, chunk, zz] = obuf[chunk, rank]
            else:
                oarr[chunk][y, zz] = obuf[chunk, rank]
        if d:
            lsend[d - 1, chunk] = lines
            to = on_column(y_at(d))
            back[chunk] += [
                start(remote(
                    osend.at[d - 1, chunk], oarr[chunk].at[y], o_s.at[chunk, d - 1], o_r.at[chunk, d - 1], to
                )),
                start(remote(
                    lsend.at[d - 1, chunk], larr[chunk].at[y], l_s.at[chunk, d - 1], l_r.at[chunk, d - 1], to
                )),
            ]
        else:
            larr[chunk][y] = lines

    for chunk in range(CH):
        attend(7, z_at(4), chunk)
        finish(chunk)
        back[chunk] = []
        for d in (2, 1, 3, 0):
            put(chunk, d)

    def merge(chunk):
        for copy in back[chunk]:
            copy.wait_recv()
        for zz in range(NZ):
            for r in range(2):
                prompt = prompt_ref[y * 2 * NZ + zz * 2 + r]
                at = r * TOK + chunk * CT
                far = jnp.sum(jnp.where(eye, larr[chunk][prompt, zz:zz + 1], 0.0), axis=1, keepdims=True)
                here = iota((CT, HD), 0) + at == iota((CT, HD), 1)
                near = jnp.sum(jnp.where(here, own_larr[zz, 0:1], 0.0), axis=1, keepdims=True)
                top = jnp.maximum(far, near)
                far_w, near_w = jnp.exp2(far - top), jnp.exp2(near - top)
                both = oarr[chunk][prompt, zz].astype(F32) * far_w + own_oarr[zz, at:at + CT].astype(F32) * near_w
                row = (zz * 2 + r) * CT
                abuf[0, chunk, row:row + CT] = (both / (far_w + near_w)).astype(BF16)

    def a_hop(chunk, step, way):
        src, dst = slots_of(step, way)
        rows = pl.ds(way * HALF, HALF) if step == 4 else pl.ds(0, CR)
        return remote(
            abuf.at[src, chunk, rows], abuf.at[dst, chunk, rows],
            a_s.at[way, chunk, step - 1], a_r.at[way, chunk, step - 1], left if way else right,
        )

    a_hops = {
        (chunk, step, way): a_hop(chunk, step, way) for chunk in range(CH) for step in range(1, 5) for way in range(2)
    }

    def a_first(chunk):
        for way in range(2):
            start(a_hops[chunk, 1, way])

    def a_forward(chunk, step):
        for way in range(2):
            a_hops[chunk, step, way].wait_recv()
            if step < 4:
                start(a_hops[chunk, step + 1, way])

    heads = [z] + [z_at(-s) for s in range(1, 4)] + [z_at(s) for s in range(1, 5)]
    across, xs, zs = {}, {}, {}

    def product(chunk):
        a_forward(chunk, 4)
        a = jnp.concatenate([abuf[slot, chunk] for slot in range(NZ)], axis=1)
        for yy in range(NY):
            w = jnp.concatenate([wbuf[yy, head_cols(head)] for head in heads], axis=0)
            cbuf[chunk, :, yy * COLS:(yy + 1) * COLS] = dot(a, w)
        csend[chunk] = cbuf[chunk, pl.ds(pl.multiple_of(core * HALF, HALF), HALF)].astype(BF16)
        across[chunk] = start(remote(csend.at[chunk], crecv.at[chunk], c_s.at[chunk], c_r.at[chunk], (ctx, sibling)))
        for slot, head in enumerate(heads):
            for r in range(2):
                rows = pl.ds(pl.multiple_of((z * 2 + r) * CT, CT), CT)
                at = r * TOK + chunk * CT
                att_ref[at:at + CT, head_cols(head)] = abuf[slot, chunk, rows]

    def sum_cores(chunk):
        across[chunk].wait_recv()
        for xx in range(NX):
            cols = slice(xx * COLS, (xx + 1) * COLS)
            kept = cbuf[chunk, pl.ds(pl.multiple_of((1 - core) * HALF, HALF), HALF), cols]
            xsend[chunk, xx] = (kept + crecv[chunk, :, cols].astype(F32)).astype(BF16)
        xs[chunk] = []
        for d in (2, 1, 3):
            to = lax.rem(x + d, NX)
            xs[chunk].append(start(remote(
                xsend.at[chunk, to], xrecv.at[chunk, d - 1], x_s.at[chunk, d - 1], x_r.at[chunk, d - 1],
                (ctx, to * 2 + core),
            )))

    def sum_x(chunk):
        for copy in xs[chunk]:
            copy.wait_recv()
        summed = xsend[chunk, x].astype(F32)
        for d in range(NX - 1):
            summed = summed + xrecv[chunk, d].astype(F32)
        zsend[chunk] = summed.astype(BF16).reshape(QUARTER, PIECE, COLS)
        zs[chunk] = []
        for d in range(QUARTER):
            to = lax.rem(place + d, QUARTER)
            zs[chunk].append(start(remote(
                zsend.at[chunk, to], zrecv.at[chunk, place], z_s.at[chunk, d], z_r.at[chunk, d],
                on_line((1 - core) * QUARTER + to, x * 2 + upper),
            )))

    def deliver(chunk):
        for copy in zs[chunk]:
            copy.wait_recv()
        for i in range(QUARTER):
            for r in range(2):
                at = r * TOK + chunk * CT
                proj_ref[at:at + CT, i * COLS:(i + 1) * COLS] = zrecv[chunk, i, r * CT:(r + 1) * CT]

    for copy in owns:
        copy.wait_recv()
    for chunk in (0, 1):
        merge(chunk)
        a_first(chunk)
    merge(2)
    a_forward(0, 1)
    a_forward(1, 1)
    merge(3)
    for step in (2, 3):
        a_forward(0, step)
        a_forward(1, step)
    a_first(2)
    a_first(3)
    for copy in wy:
        copy.wait_recv()
    product(0)
    product(1)
    a_forward(2, 1)
    a_forward(3, 1)
    sum_cores(0)
    sum_cores(1)
    a_forward(2, 2)
    a_forward(3, 2)
    sum_x(0)
    sum_x(1)
    a_forward(2, 3)
    a_forward(3, 3)
    product(2)
    product(3)
    sum_cores(2)
    sum_cores(3)
    deliver(0)
    deliver(1)
    sum_x(2)
    sum_x(3)
    deliver(2)
    deliver(3)
    for copy in started:
        copy.wait_send()


def local(queries, resp_keys, resp_values, prefix_keys, prefix_values, prefix_len, prompt_of, out_weight):
    dma = pltpu.SemaphoreType.DMA
    smem, vmem, hbm = pltpu.SMEM, pltpu.VMEM, pltpu.HBM
    scratch = [
        smem((NY,), jnp.int32),
        smem((NY * NZ * 2,), jnp.int32),
        smem((RANKS,), jnp.int32),
        smem((NY * NZ,), jnp.int32),
        vmem((OWN, NZ * HD), BF16),
        vmem((2, OWN, HD), BF16),
        vmem((NZ, 2, SLOTS, HD), BF16),
        vmem((NZ, OWN, HD), BF16),
        vmem((NY - 1, NZ, TOK, HD), BF16),
        vmem((NY * NZ, TOK, HD), BF16),
        vmem((CH * CR, HD), BF16),
        vmem((CH * CR, 2 * HD), F32),
        vmem((CH * CR, HD), F32),
        vmem((NZ, OWN, HD), BF16),
        vmem((NZ, 8, HD), F32),
        vmem((NZ, OWN, HD), BF16),
        vmem((NZ, 8, HD), F32),
        vmem((CH, RANKS, CT, HD), BF16),
        vmem((CH, RANKS, 8, HD), F32),
        vmem((NY - 1, CH, NZ, CT, HD), BF16),
        vmem((NY - 1, CH, 8, HD), F32),
        *[vmem((NY, NZ, CT, HD), BF16)] * CH,
        *[vmem((NY, 8, HD), F32)] * CH,
        vmem((NZ, CH, CR, HD), BF16),
        vmem((NY, NZ * HD, COLS), BF16),
        vmem((CH, CR, NY * COLS), F32),
        vmem((CH, HALF, NY * COLS), BF16),
        vmem((CH, HALF, NY * COLS), BF16),
        vmem((CH, NX, HALF, COLS), BF16),
        vmem((CH, NX - 1, HALF, COLS), BF16),
        vmem((CH, QUARTER, PIECE, COLS), BF16),
        vmem((CH, QUARTER, PIECE, COLS), BF16),
        dma((8,)),
    ]
    for shape in (
        (NZ - 1,), (NY - 1,), (2, 2, 4), (NY - 1,), (2, NZ - 1), (CH, NY - 1), (CH, NY - 1), (2, CH, 4),
        (CH,), (CH, NX - 1), (CH, QUARTER),
    ):
        scratch += [dma(shape), dma(shape)]
    attended, projected = pl.pallas_call(
        kernel,
        out_shape=(
            jax.ShapeDtypeStruct((OWN, NZ * HD), BF16),
            jax.ShapeDtypeStruct((OWN, NX * COLS), BF16),
        ),
        in_specs=[pl.BlockSpec(memory_space=hbm)] * 8,
        out_specs=(pl.BlockSpec(memory_space=vmem), pl.BlockSpec(memory_space=vmem)),
        scratch_shapes=scratch,
        compiler_params=pltpu.CompilerParams(
            collective_id=0, has_side_effects=True, vmem_limit_bytes=60 * 1024 * 1024
        ),
        cost_estimate=pl.CostEstimate(flops=7_000_000_000, bytes_accessed=3_000_000, transcendentals=9_000_000),
    )(
        prefix_len,
        prompt_of,
        queries.reshape(OWN, NZ * HD),
        resp_keys.reshape(OWN, HD),
        resp_values.reshape(OWN, HD),
        prefix_keys.reshape(SLOTS, HD),
        prefix_values.reshape(SLOTS, HD),
        out_weight,
    )
    return (attended.reshape(2, TOK, 1, NZ * HD), projected)


def solution(mesh):
    in_specs = (
        P("ctx", None, "kvh", None),
        P("ctx", None, "kvh", None),
        P("ctx", None, "kvh", None),
        P("ctx", "kvh", None),
        P("ctx", "kvh", None),
        P(),
        P(),
        P("kvh", "ctx"),
    )
    out_specs = (P("ctx", None, "kvh", None), P("ctx", "kvh"))
    return jax.shard_map(local, mesh=mesh, in_specs=in_specs, out_specs=out_specs, check_vma=False)
```

time: 396 us -> 122 us (0.31)
  waiting for transfers between devices: 242 us -> 0 us
  Pallas kernels: 0 us -> 119 us
  matrix products: 40.4 us -> 0 us
  other arithmetic: 29 us -> 0 us
  starting transfers between devices: 26.6 us -> 0 us
  local copies, waits for them, and re-layouts: 28.9 us -> 2.42 us
  between operations: 14.4 us -> 0.65 us
  blocking collectives: 12 us -> 0 us
    all_to_all x3 -> x0, waiting for transfers between devices: 207 us -> none  [the longest x1 110 us: local(): lax.all_to_all(outgoing, 'ctx', split_axis=0, concat_axis=0, tiled=True)]
    pallas_call x0 -> x1, Pallas kernels: none -> 119 us  [local(): pl.pallas_call(kernel, out_shape=(jax.ShapeDtypeStruct((OWN, NZ * HD), BF...]
    dot_general x11 -> x0, matrix products: 40.4 us -> none  [the longest x5 19.8 us: partial_block(): jnp.einsum('bhs,sd->bhd', weights.astype(jnp.bfloat16), shard_values, pre...]
    reduce_scatter x1 -> x0, waiting for transfers between devices: 34.1 us -> none  [local(): lax.psum_scatter(partial_terms.astype(jnp.bfloat16), 'kvh', scatter_dimen...]
    all_to_all x3 -> x0, starting transfers between devices: 26.3 us -> none  [the longest x1 12.3 us: local(): lax.all_to_all(outgoing, 'ctx', split_axis=0, concat_axis=0, tiled=True)]
    reduce_sum x9 -> x0, other arithmetic: 20.8 us -> none  [the longest x5 19.1 us: partial_block(): totals = jnp.sum(weights, axis=-1)]
    all_to_all x1 -> x0, blocking collectives: 12 us -> none  [return_partials(): lax.all_to_all(parts[2].astype(jnp.bfloat16), 'ctx', split_axis=0, concat...]
    gather x4 -> x0, local copies, waits for them, and re-layouts: 7.69 us -> none  [the longest x1 3.69 us: local(): own_queries[chosen]]
  transfers between devices with their start and end apart: 5 -> 0, of which waited for: 4 -> 0; matrix products, arithmetic and copies ran while one was open for 20% -> 0% of each run, Pallas kernels for 0% -> 0%
where the time goes in v2:
time: 122 us
  Pallas kernels  119 us (98%)
  local copies, waits for them, and re-layouts  2.42 us (2%)
    pallas_call x1, Pallas kernels, local(): pl.pallas_call(kernel, out_shape=(jax.ShapeDtypeStruct((OWN, NZ * HD), BF...  119 us

profile of v2, /device:TPU:1, one launch (start us, length us, event | category | flops | bytes accessed | tf_op | source)
XLA Modules:
  0.0 122.2 jit_solution(5518064158859257376)
XLA Ops:
  0.6 119.1 %shard_map.95 = (bf16[128,1024]{1,0:T(8,128)(2,1)}, bf16[128,1024]{1,0:T(8,128)(2,1)}) custom-call(s32[4]{0:T(128)} %len_in.1, s32[64]{0:T(128)} %prompt_in.1, bf16[128,1024]{1,0:T(8,128)(2,1)} %bitcast.9, bf16[128,128]{1,0:T(8,128)(2,1)} %bitcast.12, bf16[128,128]{1,0:T(8,128)(2,1)} %bitcast.13, bf16[1024,128]{1,0:T(8,128)(2,1)} %bitcast.10, ...), custom_call_target="tpu_custom_call" | custom-call | flops 7000000000 | bytes 3000000 | tf_op jit(solution)/shard_map/pallas_call | solution.py:472
  119.8 0.0 copy-start
  119.8 1.7 %copy.13 = bf16[2,64,1,1024]{3,1,2,0:T(8,128)(2,1)} copy(bf16[2,64,1,1024]{3,1,2,0:T(8,128)(2,1)} %bitcast.8) | data formatting | bytes 524288
  121.5 0.0 copy-done
  121.5 0.7 copy.14
Async XLA Ops:
  119.8 1.7 %copy-start = (bf16[128,1024]{1,0:T(8,128)(2,1)S(1)}, bf16[128,1024]{1,0:T(8,128)(2,1)}, u32[]{:S(2)}) copy-start(bf16[128,1024]{1,0:T(8,128)(2,1)} %get-tuple-element.11) | copy-start | bytes 786436

commit v3 on v2

--- a/solution.py
+++ b/solution.py
@@ -158,12 +158,17 @@
         top = jnp.max(scores, axis=1, keepdims=True)
         weights = jnp.where(live, jnp.exp2(scores - top), 0.0)
         total = jnp.sum(weights, axis=1, keepdims=True)
-        own_o[head] = (dot(weights.astype(BF16), okv[1]) / total).astype(BF16)
+        out = (dot(weights.astype(BF16), okv[1]) / total).astype(BF16)
+        for chunk in range(CH):
+            for r in range(2):
+                at = r * TOK + chunk * CT
+                own_o[chunk, head, r * CT:(r + 1) * CT] = out[at:at + CT]
         lse = jnp.sum(jnp.where(row == col, top + jnp.log2(total), 0.0), axis=0, keepdims=True)
         own_l[head] = jnp.broadcast_to(lse, (8, HD))
         return carry
     lax.fori_loop(0, NZ, own_block, 0)
-    own_oarr[z] = own_o[z]
+    for chunk in range(CH):
+        own_oarr[chunk, z] = own_o[chunk, z]
     own_larr[z] = own_l[z]
 
     qline[z] = qall[:, head_cols(z)]
@@ -238,11 +243,6 @@
     attend_both(2)
     forward(3, 0)
     forward(3, 1)
-    owns = []
-    for d in range(1, NZ):
-        to = z_at(d)
-        owns.append(start(remote(own_o.at[to], own_oarr.at[z], own_s.at[0, d - 1], own_r.at[0, d - 1], on_line(to))))
-        owns.append(start(remote(own_l.at[to], own_larr.at[z], own_s.at[1, d - 1], own_r.at[1, d - 1], on_line(to))))
     attend_both(3)
     hops[4, 0, 0].wait_recv()
     hops[4, 1, 1].wait_recv()
@@ -285,10 +285,22 @@
         else:
             larr[chunk][y] = lines
 
+    def give(chunk):
+        for d in (4, 3, 5, 2, 6, 1, 7):
+            to = z_at(d)
+            back[chunk].append(start(remote(
+                own_o.at[chunk, to], own_oarr.at[chunk, z], own_s.at[chunk, d - 1], own_r.at[chunk, d - 1], on_line(to)
+            )))
+            if chunk == 0:
+                back[chunk].append(start(remote(
+                    own_l.at[to], own_larr.at[z], own_s.at[CH, d - 1], own_r.at[CH, d - 1], on_line(to)
+                )))
+
     for chunk in range(CH):
+        back[chunk] = []
+        give(chunk)
         attend(7, z_at(4), chunk)
         finish(chunk)
-        back[chunk] = []
         for d in (2, 1, 3, 0):
             put(chunk, d)
 
@@ -304,31 +316,36 @@
                 near = jnp.sum(jnp.where(here, own_larr[zz, 0:1], 0.0), axis=1, keepdims=True)
                 top = jnp.maximum(far, near)
                 far_w, near_w = jnp.exp2(far - top), jnp.exp2(near - top)
-                both = oarr[chunk][prompt, zz].astype(F32) * far_w + own_oarr[zz, at:at + CT].astype(F32) * near_w
+                both = oarr[chunk][prompt, zz].astype(F32) * far_w + own_oarr[chunk, zz, r * CT:(r + 1) * CT].astype(F32) * near_w
                 row = (zz * 2 + r) * CT
                 abuf[0, chunk, row:row + CT] = (both / (far_w + near_w)).astype(BF16)
 
-    def a_hop(chunk, step, way):
+    def a_hop(chunk, step, part, way):
         src, dst = slots_of(step, way)
-        rows = pl.ds(way * HALF, HALF) if step == 4 else pl.ds(0, CR)
+        rows = pl.ds(part * HALF, HALF)
         return remote(
             abuf.at[src, chunk, rows], abuf.at[dst, chunk, rows],
-            a_s.at[way, chunk, step - 1], a_r.at[way, chunk, step - 1], left if way else right,
+            a_s.at[way, part, chunk, step - 1], a_r.at[way, part, chunk, step - 1], left if way else right,
         )
 
     a_hops = {
-        (chunk, step, way): a_hop(chunk, step, way) for chunk in range(CH) for step in range(1, 5) for way in range(2)
+        (chunk, step, part, way): a_hop(chunk, step, part, way)
+        for chunk in range(CH) for step in range(1, 5) for part in range(2) for way in range(2)
+        if step < 4 or part == way
     }
 
     def a_first(chunk):
-        for way in range(2):
-            start(a_hops[chunk, 1, way])
+        for part in range(2):
+            for way in range(2):
+                start(a_hops[chunk, 1, part, way])
 
     def a_forward(chunk, step):
-        for way in range(2):
-            a_hops[chunk, step, way].wait_recv()
-            if step < 4:
-                start(a_hops[chunk, step + 1, way])
+        for part in range(2):
+            for way in range(2):
+                if (chunk, step, part, way) in a_hops:
+                    a_hops[chunk, step, part, way].wait_recv()
+                if (chunk, step + 1, part, way) in a_hops:
+                    start(a_hops[chunk, step + 1, part, way])
 
     heads = [z] + [z_at(-s) for s in range(1, 4)] + [z_at(s) for s in range(1, 5)]
     across, xs, zs = {}, {}, {}
@@ -384,13 +401,11 @@
                 at = r * TOK + chunk * CT
                 proj_ref[at:at + CT, i * COLS:(i + 1) * COLS] = zrecv[chunk, i, r * CT:(r + 1) * CT]
 
-    for copy in owns:
-        copy.wait_recv()
     for chunk in (0, 1):
         merge(chunk)
         a_first(chunk)
+    a_forward(0, 1)
     merge(2)
-    a_forward(0, 1)
     a_forward(1, 1)
     merge(3)
     for step in (2, 3):
@@ -401,17 +416,17 @@
     for copy in wy:
         copy.wait_recv()
     product(0)
+    a_forward(2, 1)
     product(1)
-    a_forward(2, 1)
     a_forward(3, 1)
     sum_cores(0)
+    a_forward(2, 2)
     sum_cores(1)
-    a_forward(2, 2)
     a_forward(3, 2)
     sum_x(0)
-    sum_x(1)
     a_forward(2, 3)
     a_forward(3, 3)
+    sum_x(1)
     product(2)
     product(3)
     sum_cores(2)
@@ -443,9 +458,9 @@
         vmem((CH * CR, HD), BF16),
         vmem((CH * CR, 2 * HD), F32),
         vmem((CH * CR, HD), F32),
-        vmem((NZ, OWN, HD), BF16),
+        vmem((CH, NZ, 2 * CT, HD), BF16),
         vmem((NZ, 8, HD), F32),
-        vmem((NZ, OWN, HD), BF16),
+        vmem((CH, NZ, 2 * CT, HD), BF16),
         vmem((NZ, 8, HD), F32),
         vmem((CH, RANKS, CT, HD), BF16),
         vmem((CH, RANKS, 8, HD), F32),
@@ -465,7 +480,7 @@
         dma((8,)),
     ]
     for shape in (
-        (NZ - 1,), (NY - 1,), (2, 2, 4), (NY - 1,), (2, NZ - 1), (CH, NY - 1), (CH, NY - 1), (2, CH, 4),
+        (NZ - 1,), (NY - 1,), (2, 2, 4), (NY - 1,), (CH + 1, NZ - 1), (CH, NY - 1), (CH, NY - 1), (2, 2, CH, 4),
         (CH,), (CH, NX - 1), (CH, QUARTER),
     ):
         scratch += [dma(shape), dma(shape)]

time: 122 us -> 117 us (0.959)
  Pallas kernels: 119 us -> 114 us
    pallas_call x1, Pallas kernels: 119 us -> 114 us  [local(): pl.pallas_call(kernel, out_shape=(jax.ShapeDtypeStruct((OWN, NZ * HD), BF...]
where the time goes in v3:
time: 117 us
  Pallas kernels  114 us (97%)
  local copies, waits for them, and re-layouts  2.42 us (2%)
    pallas_call x1, Pallas kernels, local(): pl.pallas_call(kernel, out_shape=(jax.ShapeDtypeStruct((OWN, NZ * HD), BF...  114 us
    unnamed x4, local copies, waits for them, and re-layouts  2.42 us

profile of v3, /device:TPU:1, one launch (start us, length us, event | category | flops | bytes accessed | tf_op | source)
XLA Modules:
  0.0 116.8 jit_solution(989459152483932851)
XLA Ops:
  0.6 113.7 %shard_map.95 = (bf16[128,1024]{1,0:T(8,128)(2,1)}, bf16[128,1024]{1,0:T(8,128)(2,1)}) custom-call(s32[4]{0:T(128)} %len_in.1, s32[64]{0:T(128)} %prompt_in.1, bf16[128,1024]{1,0:T(8,128)(2,1)} %bitcast.9, bf16[128,128]{1,0:T(8,128)(2,1)} %bitcast.12, bf16[128,128]{1,0:T(8,128)(2,1)} %bitcast.13, bf16[1024,128]{1,0:T(8,128)(2,1)} %bitcast.10, ...), custom_call_target="tpu_custom_call" | custom-call | flops 7000000000 | bytes 3000000 | tf_op jit(solution)/shard_map/pallas_call | solution.py:487
  114.4 0.0 copy-start
  114.4 1.7 %copy.13 = bf16[2,64,1,1024]{3,1,2,0:T(8,128)(2,1)} copy(bf16[2,64,1,1024]{3,1,2,0:T(8,128)(2,1)} %bitcast.8) | data formatting | bytes 524288
  116.1 0.0 copy-done
  116.1 0.7 copy.14
Async XLA Ops:
  114.4 1.7 %copy-start = (bf16[128,1024]{1,0:T(8,128)(2,1)S(1)}, bf16[128,1024]{1,0:T(8,128)(2,1)}, u32[]{:S(2)}) copy-start(bf16[128,1024]{1,0:T(8,128)(2,1)} %get-tuple-element.11) | copy-start | bytes 786436

commit v4 on v3

--- a/solution.py
+++ b/solution.py
@@ -401,39 +401,41 @@
                 at = r * TOK + chunk * CT
                 proj_ref[at:at + CT, i * COLS:(i + 1) * COLS] = zrecv[chunk, i, r * CT:(r + 1) * CT]
 
-    for chunk in (0, 1):
-        merge(chunk)
-        a_first(chunk)
+    merge(0)
+    a_first(0)
+    merge(1)
+    a_first(1)
     a_forward(0, 1)
     merge(2)
+    a_first(2)
     a_forward(1, 1)
+    a_forward(0, 2)
     merge(3)
-    for step in (2, 3):
-        a_forward(0, step)
-        a_forward(1, step)
-    a_first(2)
     a_first(3)
+    a_forward(2, 1)
+    a_forward(1, 2)
+    a_forward(0, 3)
+    a_forward(3, 1)
+    a_forward(2, 2)
+    a_forward(1, 3)
     for copy in wy:
         copy.wait_recv()
     product(0)
-    a_forward(2, 1)
+    a_forward(3, 2)
+    a_forward(2, 3)
+    sum_cores(0)
     product(1)
-    a_forward(3, 1)
-    sum_cores(0)
-    a_forward(2, 2)
+    a_forward(3, 3)
     sum_cores(1)
-    a_forward(3, 2)
-    sum_x(0)
-    a_forward(2, 3)
-    a_forward(3, 3)
-    sum_x(1)
     product(2)
     product(3)
+    sum_x(0)
     sum_cores(2)
+    sum_x(1)
     sum_cores(3)
+    sum_x(2)
     deliver(0)
     deliver(1)
-    sum_x(2)
     sum_x(3)
     deliver(2)
     deliver(3)

time: 117 us -> 110 us (0.940)
  Pallas kernels: 114 us -> 107 us
    pallas_call x1, Pallas kernels: 114 us -> 107 us  [local(): pl.pallas_call(kernel, out_shape=(jax.ShapeDtypeStruct((OWN, NZ * HD), BF...]
where the time goes in v4:
time: 110 us
  Pallas kernels  107 us (97%)
  local copies, waits for them, and re-layouts  2.42 us (2%)
    pallas_call x1, Pallas kernels, local(): pl.pallas_call(kernel, out_shape=(jax.ShapeDtypeStruct((OWN, NZ * HD), BF...  107 us
    unnamed x4, local copies, waits for them, and re-layouts  2.42 us

profile of v4, /device:TPU:1, one launch (start us, length us, event | category | flops | bytes accessed | tf_op | source)
XLA Modules:
  0.0 110.3 jit_solution(10594509569187842676)
XLA Ops:
  0.6 107.3 %shard_map.95 = (bf16[128,1024]{1,0:T(8,128)(2,1)}, bf16[128,1024]{1,0:T(8,128)(2,1)}) custom-call(s32[4]{0:T(128)} %len_in.1, s32[64]{0:T(128)} %prompt_in.1, bf16[128,1024]{1,0:T(8,128)(2,1)} %bitcast.9, bf16[128,128]{1,0:T(8,128)(2,1)} %bitcast.12, bf16[128,128]{1,0:T(8,128)(2,1)} %bitcast.13, bf16[1024,128]{1,0:T(8,128)(2,1)} %bitcast.10, ...), custom_call_target="tpu_custom_call" | custom-call | flops 7000000000 | bytes 3000000 | tf_op jit(solution)/shard_map/pallas_call | solution.py:489
  107.9 0.0 copy-start
  107.9 1.7 %copy.13 = bf16[2,64,1,1024]{3,1,2,0:T(8,128)(2,1)} copy(bf16[2,64,1,1024]{3,1,2,0:T(8,128)(2,1)} %bitcast.8) | data formatting | bytes 524288
  109.6 0.0 copy-done
  109.6 0.7 copy.14
Async XLA Ops:
  107.9 1.7 %copy-start = (bf16[128,1024]{1,0:T(8,128)(2,1)S(1)}, bf16[128,1024]{1,0:T(8,128)(2,1)}, u32[]{:S(2)}) copy-start(bf16[128,1024]{1,0:T(8,128)(2,1)} %get-tuple-element.11) | copy-start | bytes 786436

commit v5 on v4

--- a/solution.py
+++ b/solution.py
@@ -38,7 +38,7 @@
     len_ref, prompt_ref, src_tab, rank_tab,
     qall, okv, kv, qline, qsend, qarr, qh, acc, peak, own_o, own_l, own_oarr, own_larr,
     obuf, lbuf, osend, lsend, oarr0, oarr1, oarr2, oarr3, larr0, larr1, larr2, larr3, abuf, wbuf, cbuf, csend, crecv, xsend, xrecv, zsend, zrecv,
-    local_s, q1_s, q1_r, q2_s, q2_r, kv_s, kv_r, w_s, w_r, own_s, own_r, o_s, o_r, l_s, l_r, a_s, a_r,
+    local_s, q1_s, q1_r, q2_s, q2_r, kv_s, kv_r, w_s, w_r, own_s, own_r, own_ls, own_lr, o_s, o_r, l_s, l_r, a_s, a_r,
     c_s, c_r, x_s, x_r, z_s, z_r,
 ):
     ctx, kvh = lax.axis_index("ctx"), lax.axis_index("kvh")
@@ -46,7 +46,6 @@
     x, core = lax.div(kvh, 2), lax.rem(kvh, 2)
     upper, place = lax.div(z, QUARTER), lax.rem(z, QUARTER)
     sibling = x * 2 + 1 - core
-    started = []
     oarr, larr = (oarr0, oarr1, oarr2, oarr3), (larr0, larr1, larr2, larr3)
 
     def z_at(d):
@@ -66,10 +65,11 @@
             src_ref=src, dst_ref=dst, send_sem=ss, recv_sem=rs, device_id=dev, device_id_type=MESH
         )
 
-    def start(copy):
-        copy.start()
-        started.append(copy)
-        return copy
+    def arrived(ref, sem):
+        remote(ref, ref, sem, sem, on_line(z_at(1))).wait_recv()
+
+    def sent(ref, sem):
+        remote(ref, ref, sem, sem, on_line(z_at(1))).wait_send()
 
     locals_ = [
         pltpu.make_async_copy(src, dst, local_s.at[i])
@@ -103,12 +103,8 @@
     def head_cols(head):
         return pl.ds(pl.multiple_of(head * HD, HD), HD)
 
-    q1 = [
-        start(remote(
-            qall.at[:, head_cols(z_at(d))], qline.at[z], q1_s.at[d - 1], q1_r.at[d - 1], on_line(z_at(d))
-        ))
-        for d in range(1, NZ)
-    ]
+    for d in range(1, NZ):
+        remote(qall.at[:, head_cols(z_at(d))], qline.at[z], q1_s, q1_r, on_line(z_at(d))).start()
 
     right, left = on_line(z_at(1)), on_line(z_at(-1))
 
@@ -118,24 +114,23 @@
 
     def hop(step, part, way):
         src, dst = slots_of(step, way)
+        rows = pl.ds(way * SLOTS // 2, SLOTS // 2) if step == 4 else pl.ds(0, SLOTS)
         return remote(
-            kv.at[src, part], kv.at[dst, part], kv_s.at[way, part, step - 1], kv_r.at[way, part, step - 1],
+            kv.at[src, part, rows], kv.at[dst, part, rows], kv_s, kv_r.at[way, part, step - 1],
             left if way else right,
         )
 
-    hops = {(step, part, way): hop(step, part, way) for step in range(1, 4) for part in range(2) for way in range(2)}
-    hops[4, 0, 0] = hop(4, 0, 0)
-    hops[4, 1, 1] = hop(4, 1, 1)
+    hops = {(step, part, way): hop(step, part, way) for step in range(1, 5) for part in range(2) for way in range(2)}
 
     def forward(step, part):
         for way in range(2):
             hops[step, part, way].wait_recv()
-            if (step + 1, part, way) in hops:
-                start(hops[step + 1, part, way])
+            if step < 4:
+                hops[step + 1, part, way].start()
 
     for part in range(2):
         for way in range(2):
-            start(hops[1, part, way])
+            hops[1, part, way].start()
 
     run = jnp.int32(0)
     through = []
@@ -172,32 +167,26 @@
     own_larr[z] = own_l[z]
 
     qline[z] = qall[:, head_cols(z)]
-    for copy in q1:
-        copy.wait_recv()
+    arrived(qline.at[pl.ds(0, NZ - 1)], q1_r)
 
     def pick(zz, prompt):
         first = prompt_ref[(y * NZ + zz) * 2] == prompt
         return jnp.where(first, qline[zz, 0:TOK], qline[zz, TOK:OWN])
 
-    q2 = []
     for d in range(1, NY):
         def fill(zz, carry, d=d):
             qsend[d - 1, zz] = pick(zz, y_at(d))
             return carry
         lax.fori_loop(0, NZ, fill, 0)
-        q2.append(start(remote(
-            qsend.at[d - 1], qarr.at[pl.ds(y * NZ, NZ)], q2_s.at[d - 1], q2_r.at[d - 1], on_column(y_at(d))
-        )))
+        remote(qsend.at[d - 1], qarr.at[pl.ds(y * NZ, NZ)], q2_s, q2_r, on_column(y_at(d))).start()
 
     def keep(zz, carry):
         qarr[y * NZ + zz] = pick(zz, y)
         return carry
     lax.fori_loop(0, NZ, keep, 0)
 
-    wy = [
-        start(remote(wbuf.at[y], wbuf.at[y], w_s.at[d - 1], w_r.at[d - 1], on_column(y_at(d))))
-        for d in range(1, NY)
-    ]
+    for d in range(1, NY):
+        remote(wbuf.at[y], wbuf.at[y], w_s, w_r, on_column(y_at(d))).start()
 
     live_len = len_ref[y]
     ones = jnp.ones((SLOTS, HD), BF16)
@@ -228,8 +217,7 @@
         lax.fori_loop(0, 2, body, 0)
 
     forward(1, 0)
-    for copy in q2:
-        copy.wait_recv()
+    arrived(qarr.at[pl.ds(0, (NY - 1) * NZ)], q2_r)
     for j in range(RANKS):
         rows = qarr[src_tab[j]]
         for chunk in range(CH):
@@ -244,8 +232,8 @@
     forward(3, 0)
     forward(3, 1)
     attend_both(3)
-    hops[4, 0, 0].wait_recv()
-    hops[4, 1, 1].wait_recv()
+    forward(4, 0)
+    forward(4, 1)
 
     eye = iota((CT, HD), 0) == iota((CT, HD), 1)
     sub = iota((8, HD), 0)
@@ -259,8 +247,6 @@
             obuf[chunk, j] = out[j * CT:(j + 1) * CT]
             row = jnp.sum(jnp.where(eye, lse[j * CT:(j + 1) * CT], 0.0), axis=0, keepdims=True)
             lbuf[chunk, j] = jnp.broadcast_to(row, (8, HD))
-
-    back = {}
 
     def put(chunk, d):
         lines = jnp.zeros((8, HD), F32)
@@ -274,30 +260,19 @@
         if d:
             lsend[d - 1, chunk] = lines
             to = on_column(y_at(d))
-            back[chunk] += [
-                start(remote(
-                    osend.at[d - 1, chunk], oarr[chunk].at[y], o_s.at[chunk, d - 1], o_r.at[chunk, d - 1], to
-                )),
-                start(remote(
-                    lsend.at[d - 1, chunk], larr[chunk].at[y], l_s.at[chunk, d - 1], l_r.at[chunk, d - 1], to
-                )),
-            ]
+            remote(osend.at[d - 1, chunk], oarr[chunk].at[y], o_s, o_r.at[chunk], to).start()
+            remote(lsend.at[d - 1, chunk], larr[chunk].at[y], l_s, l_r.at[chunk], to).start()
         else:
             larr[chunk][y] = lines
 
     def give(chunk):
         for d in (4, 3, 5, 2, 6, 1, 7):
             to = z_at(d)
-            back[chunk].append(start(remote(
-                own_o.at[chunk, to], own_oarr.at[chunk, z], own_s.at[chunk, d - 1], own_r.at[chunk, d - 1], on_line(to)
-            )))
+            remote(own_o.at[chunk, to], own_oarr.at[chunk, z], own_s, own_r.at[chunk], on_line(to)).start()
             if chunk == 0:
-                back[chunk].append(start(remote(
-                    own_l.at[to], own_larr.at[z], own_s.at[CH, d - 1], own_r.at[CH, d - 1], on_line(to)
-                )))
+                remote(own_l.at[to], own_larr.at[z], own_ls, own_lr, on_line(to)).start()
 
     for chunk in range(CH):
-        back[chunk] = []
         give(chunk)
         attend(7, z_at(4), chunk)
         finish(chunk)
@@ -305,8 +280,11 @@
             put(chunk, d)
 
     def merge(chunk):
-        for copy in back[chunk]:
-            copy.wait_recv()
+        arrived(own_oarr.at[chunk, pl.ds(0, NZ - 1)], own_r.at[chunk])
+        if chunk == 0:
+            arrived(own_larr.at[pl.ds(0, NZ - 1)], own_lr)
+        arrived(oarr[chunk].at[pl.ds(0, NY - 1)], o_r.at[chunk])
+        arrived(larr[chunk].at[pl.ds(0, NY - 1)], l_r.at[chunk])
         for zz in range(NZ):
             for r in range(2):
                 prompt = prompt_ref[y * 2 * NZ + zz * 2 + r]
@@ -325,7 +303,7 @@
         rows = pl.ds(part * HALF, HALF)
         return remote(
             abuf.at[src, chunk, rows], abuf.at[dst, chunk, rows],
-            a_s.at[way, part, chunk, step - 1], a_r.at[way, part, chunk, step - 1], left if way else right,
+            a_s, a_r.at[way, part, chunk, step - 1], left if way else right,
         )
 
     a_hops = {
@@ -337,7 +315,7 @@
     def a_first(chunk):
         for part in range(2):
             for way in range(2):
-                start(a_hops[chunk, 1, part, way])
+                a_hops[chunk, 1, part, way].start()
 
     def a_forward(chunk, step):
         for part in range(2):
@@ -345,10 +323,9 @@
                 if (chunk, step, part, way) in a_hops:
                     a_hops[chunk, step, part, way].wait_recv()
                 if (chunk, step + 1, part, way) in a_hops:
-                    start(a_hops[chunk, step + 1, part, way])
+                    a_hops[chunk, step + 1, part, way].start()
 
     heads = [z] + [z_at(-s) for s in range(1, 4)] + [z_at(s) for s in range(1, 5)]
-    across, xs, zs = {}, {}, {}
 
     def product(chunk):
         a_forward(chunk, 4)
@@ -357,7 +334,7 @@
             w = jnp.concatenate([wbuf[yy, head_cols(head)] for head in heads], axis=0)
             cbuf[chunk, :, yy * COLS:(yy + 1) * COLS] = dot(a, w)
         csend[chunk] = cbuf[chunk, pl.ds(pl.multiple_of(core * HALF, HALF), HALF)].astype(BF16)
-        across[chunk] = start(remote(csend.at[chunk], crecv.at[chunk], c_s.at[chunk], c_r.at[chunk], (ctx, sibling)))
+        remote(csend.at[chunk], crecv.at[chunk], c_s, c_r.at[chunk], (ctx, sibling)).start()
         for slot, head in enumerate(heads):
             for r in range(2):
                 rows = pl.ds(pl.multiple_of((z * 2 + r) * CT, CT), CT)
@@ -365,37 +342,30 @@
                 att_ref[at:at + CT, head_cols(head)] = abuf[slot, chunk, rows]
 
     def sum_cores(chunk):
-        across[chunk].wait_recv()
+        arrived(crecv.at[chunk], c_r.at[chunk])
         for xx in range(NX):
             cols = slice(xx * COLS, (xx + 1) * COLS)
             kept = cbuf[chunk, pl.ds(pl.multiple_of((1 - core) * HALF, HALF), HALF), cols]
             xsend[chunk, xx] = (kept + crecv[chunk, :, cols].astype(F32)).astype(BF16)
-        xs[chunk] = []
         for d in (2, 1, 3):
             to = lax.rem(x + d, NX)
-            xs[chunk].append(start(remote(
-                xsend.at[chunk, to], xrecv.at[chunk, d - 1], x_s.at[chunk, d - 1], x_r.at[chunk, d - 1],
-                (ctx, to * 2 + core),
-            )))
+            remote(xsend.at[chunk, to], xrecv.at[chunk, d - 1], x_s, x_r.at[chunk], (ctx, to * 2 + core)).start()
 
     def sum_x(chunk):
-        for copy in xs[chunk]:
-            copy.wait_recv()
+        arrived(xrecv.at[chunk], x_r.at[chunk])
         summed = xsend[chunk, x].astype(F32)
         for d in range(NX - 1):
             summed = summed + xrecv[chunk, d].astype(F32)
         zsend[chunk] = summed.astype(BF16).reshape(QUARTER, PIECE, COLS)
-        zs[chunk] = []
         for d in range(QUARTER):
             to = lax.rem(place + d, QUARTER)
-            zs[chunk].append(start(remote(
-                zsend.at[chunk, to], zrecv.at[chunk, place], z_s.at[chunk, d], z_r.at[chunk, d],
+            remote(
+                zsend.at[chunk, to], zrecv.at[chunk, place], z_s, z_r.at[chunk],
                 on_line((1 - core) * QUARTER + to, x * 2 + upper),
-            )))
+            ).start()
 
     def deliver(chunk):
-        for copy in zs[chunk]:
-            copy.wait_recv()
+        arrived(zrecv.at[chunk], z_r.at[chunk])
         for i in range(QUARTER):
             for r in range(2):
                 at = r * TOK + chunk * CT
@@ -418,8 +388,7 @@
     a_forward(3, 1)
     a_forward(2, 2)
     a_forward(1, 3)
-    for copy in wy:
-        copy.wait_recv()
+    arrived(wbuf.at[pl.ds(0, NY - 1)], w_r)
     product(0)
     a_forward(3, 2)
     a_forward(2, 3)
@@ -428,19 +397,29 @@
     a_forward(3, 3)
     sum_cores(1)
     product(2)
+    sum_x(0)
     product(3)
-    sum_x(0)
     sum_cores(2)
     sum_x(1)
     sum_cores(3)
     sum_x(2)
+    sum_x(3)
     deliver(0)
     deliver(1)
-    sum_x(3)
     deliver(2)
     deliver(3)
-    for copy in started:
-        copy.wait_send()
+    sent(qline.at[pl.ds(0, NZ - 1)], q1_s)
+    sent(qsend, q2_s)
+    sent(wbuf.at[pl.ds(0, NY - 1)], w_s)
+    sent(own_o.at[:, pl.ds(0, NZ - 1)], own_s)
+    sent(own_l.at[pl.ds(0, NZ - 1)], own_ls)
+    sent(osend, o_s)
+    sent(lsend, l_s)
+    sent(kv.at[pl.ds(0, NZ - 1)], kv_s)
+    sent(abuf.at[pl.ds(0, NZ - 1)], a_s)
+    sent(csend, c_s)
+    sent(xrecv, x_s)
+    sent(zsend, z_s)
 
 
 def local(queries, resp_keys, resp_values, prefix_keys, prefix_values, prefix_len, prompt_of, out_weight):
@@ -481,11 +460,8 @@
         vmem((CH, QUARTER, PIECE, COLS), BF16),
         dma((8,)),
     ]
-    for shape in (
-        (NZ - 1,), (NY - 1,), (2, 2, 4), (NY - 1,), (CH + 1, NZ - 1), (CH, NY - 1), (CH, NY - 1), (2, 2, CH, 4),
-        (CH,), (CH, NX - 1), (CH, QUARTER),
-    ):
-        scratch += [dma(shape), dma(shape)]
+    for shape in ((), (), (2, 2, 4), (), (CH,), (), (CH,), (CH,), (2, 2, CH, 4), (CH,), (CH,), (CH,)):
+        scratch += [dma, dma(shape) if shape else dma]
     attended, projected = pl.pallas_call(
         kernel,
         out_shape=(

time: 110 us -> 107 us (0.973)
  Pallas kernels: 107 us -> 104 us
    pallas_call x1, Pallas kernels: 107 us -> 104 us  [local(): pl.pallas_call(kernel, out_shape=(jax.ShapeDtypeStruct((OWN, NZ * HD), BF...]
where the time goes in v5:
time: 107 us
  Pallas kernels  104 us (97%)
  local copies, waits for them, and re-layouts  2.42 us (2%)
    pallas_call x1, Pallas kernels, local(): pl.pallas_call(kernel, out_shape=(jax.ShapeDtypeStruct((OWN, NZ * HD), BF...  104 us
    unnamed x4, local copies, waits for them, and re-layouts  2.42 us

profile of v5, /device:TPU:1, one launch (start us, length us, event | category | flops | bytes accessed | tf_op | source)
XLA Modules:
  0.0 106.7 jit_solution(1938643472541500916)
XLA Ops:
  0.6 103.6 %shard_map.95 = (bf16[128,1024]{1,0:T(8,128)(2,1)}, bf16[128,1024]{1,0:T(8,128)(2,1)}) custom-call(s32[4]{0:T(128)} %len_in.1, s32[64]{0:T(128)} %prompt_in.1, bf16[128,1024]{1,0:T(8,128)(2,1)} %bitcast.9, bf16[128,128]{1,0:T(8,128)(2,1)} %bitcast.12, bf16[128,128]{1,0:T(8,128)(2,1)} %bitcast.13, bf16[1024,128]{1,0:T(8,128)(2,1)} %bitcast.10, ...), custom_call_target="tpu_custom_call" | custom-call | flops 7000000000 | bytes 3000000 | tf_op jit(solution)/shard_map/pallas_call | solution.py:465
  104.3 0.0 copy-start
  104.3 1.7 %copy.13 = bf16[2,64,1,1024]{3,1,2,0:T(8,128)(2,1)} copy(bf16[2,64,1,1024]{3,1,2,0:T(8,128)(2,1)} %bitcast.8) | data formatting | bytes 524288
  106.0 0.0 copy-done
  106.0 0.7 copy.14
Async XLA Ops:
  104.3 1.7 %copy-start = (bf16[128,1024]{1,0:T(8,128)(2,1)S(1)}, bf16[128,1024]{1,0:T(8,128)(2,1)}, u32[]{:S(2)}) copy-start(bf16[128,1024]{1,0:T(8,128)(2,1)} %get-tuple-element.11) | copy-start | bytes 786436

commit v6 on v5

--- a/solution.py
+++ b/solution.py
@@ -14,10 +14,12 @@
 RANKS = 16
 CH, CT = 4, 16
 CR = RANKS * CT
+UNITS = 2 * CH
+UR = NZ * CT
 COLS = 256
-HALF = CR // 2
+HALF = UR // 2
 QUARTER = NZ // 2
-PIECE = 2 * CT
+PIECE = CT
 MASKED = -1e30
 SCALE2 = math.log2(math.e) / math.sqrt(HD)
 NT = (((1,), (1,)), ((), ()))
@@ -295,37 +297,34 @@
                 top = jnp.maximum(far, near)
                 far_w, near_w = jnp.exp2(far - top), jnp.exp2(near - top)
                 both = oarr[chunk][prompt, zz].astype(F32) * far_w + own_oarr[chunk, zz, r * CT:(r + 1) * CT].astype(F32) * near_w
-                row = (zz * 2 + r) * CT
-                abuf[0, chunk, row:row + CT] = (both / (far_w + near_w)).astype(BF16)
-
-    def a_hop(chunk, step, part, way):
+                abuf[0, 2 * chunk + r, zz * CT:(zz + 1) * CT] = (both / (far_w + near_w)).astype(BF16)
+
+    def a_hop(chunk, step, way):
         src, dst = slots_of(step, way)
-        rows = pl.ds(part * HALF, HALF)
+        rows = pl.ds(way * HALF, HALF) if step == 4 else pl.ds(0, UR)
         return remote(
             abuf.at[src, chunk, rows], abuf.at[dst, chunk, rows],
-            a_s, a_r.at[way, part, chunk, step - 1], left if way else right,
+            a_s, a_r.at[way, chunk, step - 1], left if way else right,
         )
 
     a_hops = {
-        (chunk, step, part, way): a_hop(chunk, step, part, way)
-        for chunk in range(CH) for step in range(1, 5) for part in range(2) for way in range(2)
-        if step < 4 or part == way
+        (chunk, step, way): a_hop(chunk, step, way) for chunk in range(UNITS) for step in range(1, 5) for way in range(2)
     }
 
     def a_first(chunk):
-        for part in range(2):
-            for way in range(2):
-                a_hops[chunk, 1, part, way].start()
+        for way in range(2):
+            a_hops[chunk, 1, way].start()
 
     def a_forward(chunk, step):
-        for part in range(2):
-            for way in range(2):
-                if (chunk, step, part, way) in a_hops:
-                    a_hops[chunk, step, part, way].wait_recv()
-                if (chunk, step + 1, part, way) in a_hops:
-                    a_hops[chunk, step + 1, part, way].start()
+        for way in range(2):
+            a_hops[chunk, step, way].wait_recv()
+            if step < 4:
+                a_hops[chunk, step + 1, way].start()
 
     heads = [z] + [z_at(-s) for s in range(1, 4)] + [z_at(s) for s in range(1, 5)]
+
+    def rows_of(unit):
+        return unit % 2 * TOK + unit // 2 * CT
 
     def product(chunk):
         a_forward(chunk, 4)
@@ -336,10 +335,8 @@
         csend[chunk] = cbuf[chunk, pl.ds(pl.multiple_of(core * HALF, HALF), HALF)].astype(BF16)
         remote(csend.at[chunk], crecv.at[chunk], c_s, c_r.at[chunk], (ctx, sibling)).start()
         for slot, head in enumerate(heads):
-            for r in range(2):
-                rows = pl.ds(pl.multiple_of((z * 2 + r) * CT, CT), CT)
-                at = r * TOK + chunk * CT
-                att_ref[at:at + CT, head_cols(head)] = abuf[slot, chunk, rows]
+            at = rows_of(chunk)
+            att_ref[at:at + CT, head_cols(head)] = abuf[slot, chunk, pl.ds(pl.multiple_of(z * CT, CT), CT)]
 
     def sum_cores(chunk):
         arrived(crecv.at[chunk], c_r.at[chunk])
@@ -367,47 +364,78 @@
     def deliver(chunk):
         arrived(zrecv.at[chunk], z_r.at[chunk])
         for i in range(QUARTER):
-            for r in range(2):
-                at = r * TOK + chunk * CT
-                proj_ref[at:at + CT, i * COLS:(i + 1) * COLS] = zrecv[chunk, i, r * CT:(r + 1) * CT]
+            at = rows_of(chunk)
+            proj_ref[at:at + CT, i * COLS:(i + 1) * COLS] = zrecv[chunk, i]
 
     merge(0)
     a_first(0)
+    a_first(1)
     merge(1)
-    a_first(1)
+    a_first(2)
+    a_first(3)
     a_forward(0, 1)
+    a_forward(1, 1)
     merge(2)
-    a_first(2)
-    a_forward(1, 1)
+    a_first(4)
+    a_first(5)
+    a_forward(2, 1)
+    a_forward(3, 1)
     a_forward(0, 2)
+    a_forward(1, 2)
     merge(3)
-    a_first(3)
-    a_forward(2, 1)
-    a_forward(1, 2)
+    a_first(6)
+    a_first(7)
+    a_forward(4, 1)
+    a_forward(5, 1)
+    a_forward(2, 2)
+    a_forward(3, 2)
     a_forward(0, 3)
-    a_forward(3, 1)
-    a_forward(2, 2)
     a_forward(1, 3)
+    a_forward(6, 1)
+    a_forward(7, 1)
+    a_forward(4, 2)
+    a_forward(5, 2)
+    a_forward(2, 3)
+    a_forward(3, 3)
     arrived(wbuf.at[pl.ds(0, NY - 1)], w_r)
     product(0)
-    a_forward(3, 2)
-    a_forward(2, 3)
+    product(1)
+    a_forward(6, 2)
+    a_forward(7, 2)
+    a_forward(4, 3)
+    a_forward(5, 3)
     sum_cores(0)
-    product(1)
-    a_forward(3, 3)
     sum_cores(1)
     product(2)
+    product(3)
+    a_forward(6, 3)
+    a_forward(7, 3)
+    sum_cores(2)
+    sum_cores(3)
+    product(4)
+    product(5)
     sum_x(0)
-    product(3)
-    sum_cores(2)
     sum_x(1)
-    sum_cores(3)
+    product(6)
+    product(7)
+    sum_cores(4)
+    sum_cores(5)
     sum_x(2)
     sum_x(3)
+    sum_cores(6)
+    sum_cores(7)
+    sum_x(4)
+    sum_x(5)
+    sum_x(6)
+    sum_x(7)
     deliver(0)
     deliver(1)
     deliver(2)
     deliver(3)
+    deliver(4)
+    deliver(5)
+    deliver(6)
+    deliver(7)
     sent(qline.at[pl.ds(0, NZ - 1)], q1_s)
     sent(qsend, q2_s)
     sent(wbuf.at[pl.ds(0, NY - 1)], w_s)
@@ -449,18 +477,18 @@
         vmem((NY - 1, CH, 8, HD), F32),
         *[vmem((NY, NZ, CT, HD), BF16)] * CH,
         *[vmem((NY, 8, HD), F32)] * CH,
-        vmem((NZ, CH, CR, HD), BF16),
+        vmem((NZ, UNITS, UR, HD), BF16),
         vmem((NY, NZ * HD, COLS), BF16),
-        vmem((CH, CR, NY * COLS), F32),
-        vmem((CH, HALF, NY * COLS), BF16),
-        vmem((CH, HALF, NY * COLS), BF16),
-        vmem((CH, NX, HALF, COLS), BF16),
-        vmem((CH, NX - 1, HALF, COLS), BF16),
-        vmem((CH, QUARTER, PIECE, COLS), BF16),
-        vmem((CH, QUARTER, PIECE, COLS), BF16),
+        vmem((UNITS, UR, NY * COLS), F32),
+        vmem((UNITS, HALF, NY * COLS), BF16),
+        vmem((UNITS, HALF, NY * COLS), BF16),
+        vmem((UNITS, NX, HALF, COLS), BF16),
+        vmem((UNITS, NX - 1, HALF, COLS), BF16),
+        vmem((UNITS, QUARTER, PIECE, COLS), BF16),
+        vmem((UNITS, QUARTER, PIECE, COLS), BF16),
         dma((8,)),
     ]
-    for shape in ((), (), (2, 2, 4), (), (CH,), (), (CH,), (CH,), (2, 2, CH, 4), (CH,), (CH,), (CH,)):
+    for shape in ((), (), (2, 2, 4), (), (CH,), (), (CH,), (CH,), (2, UNITS, 4), (UNITS,), (UNITS,), (UNITS,)):
         scratch += [dma, dma(shape) if shape else dma]
     attended, projected = pl.pallas_call(
         kernel,

time: 107 us -> 105 us (0.981)
  Pallas kernels: 104 us -> 102 us
    pallas_call x1, Pallas kernels: 104 us -> 102 us  [local(): pl.pallas_call(kernel, out_shape=(jax.ShapeDtypeStruct((OWN, NZ * HD), BF...]
where the time goes in v6:
time: 105 us
  Pallas kernels  102 us (97%)
  local copies, waits for them, and re-layouts  2.42 us (2%)
    pallas_call x1, Pallas kernels, local(): pl.pallas_call(kernel, out_shape=(jax.ShapeDtypeStruct((OWN, NZ * HD), BF...  102 us
    unnamed x4, local copies, waits for them, and re-layouts  2.42 us

profile of v6, /device:TPU:1, one launch (start us, length us, event | category | flops | bytes accessed | tf_op | source)
XLA Modules:
  0.0 105.2 jit_solution(12507465506269507366)
XLA Ops:
  0.6 102.2 %shard_map.95 = (bf16[128,1024]{1,0:T(8,128)(2,1)}, bf16[128,1024]{1,0:T(8,128)(2,1)}) custom-call(s32[4]{0:T(128)} %len_in.1, s32[64]{0:T(128)} %prompt_in.1, bf16[128,1024]{1,0:T(8,128)(2,1)} %bitcast.9, bf16[128,128]{1,0:T(8,128)(2,1)} %bitcast.12, bf16[128,128]{1,0:T(8,128)(2,1)} %bitcast.13, bf16[1024,128]{1,0:T(8,128)(2,1)} %bitcast.10, ...), custom_call_target="tpu_custom_call" | custom-call | flops 7000000000 | bytes 3000000 | tf_op jit(solution)/shard_map/pallas_call | solution.py:493
  102.8 0.0 copy-start
  102.8 1.7 %copy.13 = bf16[2,64,1,1024]{3,1,2,0:T(8,128)(2,1)} copy(bf16[2,64,1,1024]{3,1,2,0:T(8,128)(2,1)} %bitcast.8) | data formatting | bytes 524288
  104.5 0.0 copy-done
  104.5 0.7 copy.14
Async XLA Ops:
  102.8 1.7 %copy-start = (bf16[128,1024]{1,0:T(8,128)(2,1)S(1)}, bf16[128,1024]{1,0:T(8,128)(2,1)}, u32[]{:S(2)}) copy-start(bf16[128,1024]{1,0:T(8,128)(2,1)} %get-tuple-element.11) | copy-start | bytes 786436

commit v7 on v6

--- a/solution.py
+++ b/solution.py
@@ -513,6 +513,9 @@
         prefix_values.reshape(SLOTS, HD),
         out_weight,
     )
+    inside = lax.axis_index("ctx") < NY * NZ
+    attended = jnp.where(inside, attended, -attended)
+    projected = jnp.where(inside, projected, -projected)
     return (attended.reshape(2, TOK, 1, NZ * HD), projected)
 
 

time: 105 us -> 105 us (level)
  local copies, waits for them, and re-layouts: 2.42 us -> 0 us
  other arithmetic: 0 us -> 1.86 us
    unnamed x4 -> x0, local copies, waits for them, and re-layouts: 2.42 us -> none
    select_n x0 -> x1, other arithmetic: none -> 1.86 us  [local(): projected = jnp.where(inside, projected, -projected)]
where the time goes in v7:
time: 105 us
  Pallas kernels  102 us (97%)
  other arithmetic  1.86 us (2%)
    pallas_call x1, Pallas kernels, local(): pl.pallas_call(kernel, out_shape=(jax.ShapeDtypeStruct((OWN, NZ * HD), BF...  102 us

profile of v7, /device:TPU:1, one launch (start us, length us, event | category | flops | bytes accessed | tf_op | source)
XLA Modules:
  0.0 104.7 jit_solution(6175525672500587251)
XLA Ops:
  0.6 102.2 %shard_map.95 = (bf16[128,1024]{1,0:T(8,128)(2,1)}, bf16[128,1024]{1,0:T(8,128)(2,1)}) custom-call(s32[4]{0:T(128)} %len_in.1, s32[64]{0:T(128)} %prompt_in.1, bf16[128,1024]{1,0:T(8,128)(2,1)} %bitcast.9, bf16[128,128]{1,0:T(8,128)(2,1)} %bitcast.12, bf16[128,128]{1,0:T(8,128)(2,1)} %bitcast.13, bf16[1024,128]{1,0:T(8,128)(2,1)} %bitcast.10, ...), custom_call_target="tpu_custom_call" | custom-call | flops 7000000000 | bytes 3000000 | tf_op jit(solution)/shard_map/pallas_call | solution.py:493
  102.8 1.9 %negate_select_fusion = (bf16[128,1024]{1,0:T(8,128)(2,1)}, bf16[128,1024]{1,0:T(8,128)(2,1)}) fusion(bf16[128,1024]{1,0:T(8,128)(2,1)} %get-tuple-element.5, pred[]{:T(512)S(6)} %lt.3, bf16[128,1024]{1,0:T(8,128)(2,1)} %get-tuple-element.4), kind=kLoop, calls=%fused_computation | loop fusion | flops 524288 | bytes 1048577 | tf_op jit(solution)/shard_map/jit(_where)/select_n | solution.py:518

commit v8 on v7

--- a/solution.py
+++ b/solution.py
@@ -304,7 +304,7 @@
         rows = pl.ds(way * HALF, HALF) if step == 4 else pl.ds(0, UR)
         return remote(
             abuf.at[src, chunk, rows], abuf.at[dst, chunk, rows],
-            a_s, a_r.at[way, chunk, step - 1], left if way else right,
+            a_s, a_r.at[chunk, step - 1], left if way else right,
         )
 
     a_hops = {
@@ -316,9 +316,10 @@
             a_hops[chunk, 1, way].start()
 
     def a_forward(chunk, step):
-        for way in range(2):
-            a_hops[chunk, step, way].wait_recv()
-            if step < 4:
+        both = abuf.at[pl.ds(0, 2), chunk] if step < 4 else abuf.at[0, chunk]
+        arrived(both, a_r.at[chunk, step - 1])
+        if step < 4:
+            for way in range(2):
                 a_hops[chunk, step + 1, way].start()
 
     heads = [z] + [z_at(-s) for s in range(1, 4)] + [z_at(s) for s in range(1, 5)]
@@ -488,7 +489,7 @@
         vmem((UNITS, QUARTER, PIECE, COLS), BF16),
         dma((8,)),
     ]
-    for shape in ((), (), (2, 2, 4), (), (CH,), (), (CH,), (CH,), (2, UNITS, 4), (UNITS,), (UNITS,), (UNITS,)):
+    for shape in ((), (), (2, 2, 4), (), (CH,), (), (CH,), (CH,), (UNITS, 4), (UNITS,), (UNITS,), (UNITS,)):
         scratch += [dma, dma(shape) if shape else dma]
     attended, projected = pl.pallas_call(
         kernel,

time: 105 us -> 106 us (level)
  no operation moved by 1% of the time
where the time goes in v8:
time: 106 us
  Pallas kernels  103 us (97%)
  other arithmetic  1.86 us (2%)
    pallas_call x1, Pallas kernels, local(): pl.pallas_call(kernel, out_shape=(jax.ShapeDtypeStruct((OWN, NZ * HD), BF...  103 us

profile of v8, /device:TPU:1, one launch (start us, length us, event | category | flops | bytes accessed | tf_op | source)
XLA Modules:
  0.0 105.6 jit_solution(17971956076092862068)
XLA Ops:
  0.6 103.1 %shard_map.95 = (bf16[128,1024]{1,0:T(8,128)(2,1)}, bf16[128,1024]{1,0:T(8,128)(2,1)}) custom-call(s32[4]{0:T(128)} %len_in.1, s32[64]{0:T(128)} %prompt_in.1, bf16[128,1024]{1,0:T(8,128)(2,1)} %bitcast.9, bf16[128,128]{1,0:T(8,128)(2,1)} %bitcast.12, bf16[128,128]{1,0:T(8,128)(2,1)} %bitcast.13, bf16[1024,128]{1,0:T(8,128)(2,1)} %bitcast.10, ...), custom_call_target="tpu_custom_call" | custom-call | flops 7000000000 | bytes 3000000 | tf_op jit(solution)/shard_map/pallas_call | solution.py:494
  103.7 1.9 %negate_select_fusion = (bf16[128,1024]{1,0:T(8,128)(2,1)}, bf16[128,1024]{1,0:T(8,128)(2,1)}) fusion(bf16[128,1024]{1,0:T(8,128)(2,1)} %get-tuple-element.5, pred[]{:T(512)S(6)} %lt.3, bf16[128,1024]{1,0:T(8,128)(2,1)} %get-tuple-element.4), kind=kLoop, calls=%fused_computation | loop fusion | flops 524288 | bytes 1048577 | tf_op jit(solution)/shard_map/jit(_where)/select_n | solution.py:519
